TPU v7x, 32 devices: a whole 2x2x4 slice. The times are simulated.
32 devices in a mesh: pixel: 4 (over y, core), crop: 2 (over x), member: 4 (over z).
Axes of the slice: x: 2, y: 2, z: 4, core: 2. Of those that a mesh axis runs over, the one named last changes fastest.
Arguments:
- forcing: bfloat16 [52, 8, 3072], P(None, None, ('pixel', 'crop')), may hold values from -6 to 6
- observed: bfloat16 [52, 3072], P(None, ('pixel', 'crop')), may hold values from -6 to 6
- obs_sigma: float32 [3072], P(('pixel', 'crop')), may hold values from 0.5 to 2
- pixel_class: int32 [3072, 1], P(('pixel', 'crop')), may hold values from 0 to 63; in each aligned block of 384 rows (0 to 383, 384 to 767, ...) at most 8 rows name the same one
- pixel_count: int32 [96], P(('pixel', 'crop')), may hold values from 16 to 32
- cloud_free: int32 [96, 52], P(('pixel', 'crop')), may hold values 0 or 1
- params: float32 [16, 8, 24], P('member'), may hold values from -6 to 6
- input_weight: bfloat16 [8, 48, 32], P('crop'), may hold values from -1 to 1
- conv_weight: bfloat16 [8, 3, 48, 96], P('crop'), may hold values from -0.625 to 0.625
- mix_weight: bfloat16 [8, 3, 48, 48], P('crop'), may hold values from -0.875 to 0.875
- head_weight: bfloat16 [8, 48], P('crop'), may hold values from -0.875 to 0.875
Outputs:
- updated: float32 [16, 8, 24], P('member', 'crop')
Inputs may be any that keep to these rules, and one draw needn't show every extreme that they name: pixel_class is crop * 8 + region; among the 384 pixel places of one pixel and crop index no class is named more than 8 times, a bound that some block reaches. `cloud_free`: 1 where the block is seen in that week.
All inputs are finite; a program needn't handle non-finite values.
Results may differ from a plain program's by a relative error of at most 0.0067.
Values may be sent and summed in bfloat16 or wider, within the bound.
No kernel may reach another device: no remote copies, remote signals or barrier semaphores. Data moves between devices by JAX's collectives and lax.ppermute only.
A program may use at most 128 MiB of HBM per device.

v0:
```python
import math

import jax
import jax.numpy as jnp
from jax import lax
from jax.sharding import PartitionSpec as P

REGIONS = 8
CAP = 8


ALPHA_INFLATION = 4.0


def pack_slots(
    forcing, observed, obs_sigma, pixel_class, pixel_count, cloud_free, n_class, cap_slots
):
    n_blocks = pixel_count.shape[0]
    n_pixels = obs_sigma.shape[0]
    block_len = n_pixels // n_blocks
    classes = pixel_class[:, 0]
    position = jnp.arange(n_pixels, dtype=jnp.int32)
    is_live = position % block_len < jnp.repeat(
        pixel_count, block_len, total_repeat_length=n_pixels
    )
    earlier = (
        (classes[None, :] == classes[:, None])
        & is_live[None, :]
        & (position[None, :] < position[:, None])
    )
    rank_in = jnp.sum(earlier.astype(jnp.int32), axis=1)
    slot_of = classes * cap_slots + rank_in
    places = jnp.arange(n_class * cap_slots, dtype=jnp.int32)
    select = ((slot_of[:, None] == places[None, :]) & is_live[:, None]).astype(jnp.bfloat16)
    seen_mask = jnp.repeat(cloud_free, block_len, axis=0, total_repeat_length=n_pixels).astype(
        jnp.float32
    )
    obs_weight = (jnp.transpose(seen_mask) / obs_sigma[None, :]).astype(jnp.bfloat16)
    obs_pair = jnp.stack([observed, obs_weight], axis=1)
    sent_forcing = jnp.einsum(
        "tfx,xs->tfs", forcing, select, preferred_element_type=jnp.float32
    ).astype(jnp.bfloat16)
    sent_pair = jnp.einsum(
        "tfx,xs->tfs", obs_pair, select, preferred_element_type=jnp.float32
    ).astype(jnp.bfloat16)
    return (sent_forcing, sent_pair)


def run_network(
    slot_forcing, theta_member, region_hot, input_weight, conv_weight, mix_weight, head_weight
):
    n_weeks = slot_forcing.shape[0]
    n_forcing = slot_forcing.shape[1]
    n_channels = conv_weight.shape[2]
    theta_bf = theta_member.astype(jnp.bfloat16)
    param_term = jnp.einsum(
        "kcp,rp->ckr", input_weight[:, :, n_forcing:], theta_bf, preferred_element_type=jnp.float32
    )
    param_slot = jnp.sum(param_term[:, :, :, None] * region_hot[None, None, :, :], axis=2)
    hidden = jnp.einsum(
        "kcf,tfkq->tckq",
        input_weight[:, :, :n_forcing],
        slot_forcing,
        preferred_element_type=jnp.float32,
    )
    hidden = (hidden + param_slot[None]).astype(jnp.bfloat16)
    for layer in range(conv_weight.shape[1]):
        dilation = 2**layer
        delayed = jnp.concatenate(
            [jnp.zeros((dilation,) + hidden.shape[1:], jnp.bfloat16), hidden[: n_weeks - dilation]],
            axis=0,
        )
        inner = jnp.einsum(
            "koc,tckq->tokq",
            conv_weight[:, layer, :, :n_channels],
            hidden,
            preferred_element_type=jnp.float32,
        )
        inner = inner + jnp.einsum(
            "koc,tckq->tokq",
            conv_weight[:, layer, :, n_channels:],
            delayed,
            preferred_element_type=jnp.float32,
        )
        inner = jax.nn.relu(inner).astype(jnp.bfloat16)
        mixed = jnp.einsum(
            "koc,tckq->tokq", mix_weight[:, layer], inner, preferred_element_type=jnp.float32
        )
        hidden = (hidden.astype(jnp.float32) + mixed).astype(jnp.bfloat16)
    return jnp.einsum("kc,tckq->tkq", head_weight, hidden, preferred_element_type=jnp.float32)


def local(
    forcing,
    observed,
    obs_sigma,
    pixel_class,
    pixel_count,
    cloud_free,
    params,
    input_weight,
    conv_weight,
    mix_weight,
    head_weight,
):
    n_crop = lax.axis_size("crop")
    n_member = lax.axis_size("member")
    n_weeks = forcing.shape[0]
    n_forcing = forcing.shape[1]
    local_crops = input_weight.shape[0]
    all_crops = local_crops * n_crop
    per_class = REGIONS * CAP
    sent_forcing, sent_pair = pack_slots(
        forcing, observed, obs_sigma, pixel_class, pixel_count, cloud_free, all_crops * REGIONS, CAP
    )
    split_forcing = sent_forcing.reshape(n_weeks, n_forcing, n_crop, local_crops, per_class)
    split_pair = sent_pair.reshape(n_weeks, 2, n_crop, local_crops, per_class)
    got_forcing, got_pair = (
        lax.all_to_all(split_forcing, "crop", split_axis=2, concat_axis=4, tiled=True),
        lax.all_to_all(split_pair, "crop", split_axis=2, concat_axis=4, tiled=True),
    )
    slot_forcing = got_forcing.reshape(n_weeks, n_forcing, local_crops, n_crop * per_class)
    slot_pair = got_pair.reshape(n_weeks, 2, -1)
    model_input, model_conv, model_mix, model_head = (
        input_weight,
        conv_weight,
        mix_weight,
        head_weight,
    )
    width_q = slot_forcing.shape[3]
    region_ids = jnp.arange(REGIONS, dtype=jnp.int32)
    region_hot = (
        jnp.arange(width_q, dtype=jnp.int32) // CAP % REGIONS == region_ids[:, None]
    ).astype(jnp.float32)

    def run_member(theta_member):
        return run_network(
            slot_forcing, theta_member, region_hot, model_input, model_conv, model_mix, model_head
        )

    my_members = params.shape[0]
    members = my_members * n_member
    predicted = lax.map(run_member, params).reshape(my_members, n_weeks, -1)
    n_slots = predicted.shape[2]
    mean_pred = lax.psum(jnp.sum(predicted, axis=0), "member") / members
    obs_value = slot_pair[:, 0].astype(jnp.float32)
    obs_weight = slot_pair[:, 1].astype(jnp.float32)
    scaled = (
        obs_weight[None]
        * (predicted - mean_pred[None])
        / math.sqrt(ALPHA_INFLATION * (members - 1))
    ).astype(jnp.bfloat16)
    innovation = obs_weight * (obs_value - mean_pred) / math.sqrt(ALPHA_INFLATION)
    slot_region = jnp.arange(n_slots, dtype=jnp.int32) // CAP % REGIONS
    zero_bf = jnp.zeros((), jnp.bfloat16)
    region_mask = slot_region[None, :] == region_ids[:, None]
    masked = jnp.where(region_mask[:, None, None, :], scaled[None], zero_bf).reshape(
        REGIONS * my_members, -1
    )
    shard_rows = lax.all_gather(scaled, "member", axis=0, tiled=True)
    flat_shard = shard_rows.reshape(shard_rows.shape[0], -1)
    gram_rows = jnp.einsum(
        "ax,bx->ab", masked, flat_shard, preferred_element_type=jnp.float32
    ).reshape(REGIONS, my_members, -1)
    innov_region = jnp.where(region_mask[:, None, :], innovation[None], 0.0).reshape(REGIONS, -1)
    proj_rows = jnp.einsum(
        "mx,rx->rm",
        scaled.reshape(my_members, -1).astype(jnp.float32),
        innov_region,
        precision=lax.Precision.HIGHEST,
    )
    owned_regions = REGIONS // n_crop
    first_region = lax.axis_index("crop") * owned_regions
    gram_sum, proj_sum = lax.psum((gram_rows, proj_rows), ("pixel", "crop"))
    gram_mine = lax.dynamic_slice_in_dim(gram_sum, first_region, owned_regions, 0)
    proj_mine = lax.dynamic_slice_in_dim(proj_sum, first_region, owned_regions, 0)
    theta_mine = lax.dynamic_slice_in_dim(params, first_region, owned_regions, 1)
    gram_full, proj_full, theta_all = (
        lax.all_gather(gram_mine, "member", axis=1, tiled=True),
        lax.all_gather(proj_mine, "member", axis=1, tiled=True),
        lax.all_gather(theta_mine, "member", axis=0, tiled=True),
    )
    first_col = lax.axis_index("member") * my_members
    scale_root = math.sqrt(members - 1)

    def update(gram_block, proj_block, theta_region, theta_own):
        system = gram_block + jnp.eye(members, dtype=jnp.float32)
        factor = jnp.linalg.cholesky(system)
        columns = lax.dynamic_slice_in_dim(gram_block, first_col, my_members, 1)
        right_side = proj_block[:, None] - scale_root * columns
        mixing = jax.scipy.linalg.cho_solve((factor, True), right_side)
        spread = (theta_region - jnp.sum(theta_region, axis=0) / members) / scale_root
        return theta_own + jnp.dot(jnp.transpose(mixing), spread, precision=lax.Precision.HIGHEST)

    return jax.vmap(update, in_axes=(0, 0, 1, 1), out_axes=1)(
        gram_full, proj_full, theta_all, theta_mine
    )


def solution(mesh):
    in_specs = (
        P(None, None, ("pixel", "crop")),
        P(None, ("pixel", "crop")),
        P(("pixel", "crop")),
        P(("pixel", "crop"), None),
        P(("pixel", "crop")),
        P(("pixel", "crop"), None),
        P("member", None, None),
        P("crop", None, None),
        P("crop", None, None, None),
        P("crop", None, None, None),
        P("crop", None),
    )
    out_specs = P("member", "crop", None)
    return jax.shard_map(local, mesh=mesh, in_specs=in_specs, out_specs=out_specs, check_vma=False)
```

profile of v0, /device:TPU:0, one launch (start us, length us, event | category | flops | bytes accessed | tf_op | source)
XLA Modules:
  0.0 366.1 jit_solution(6848459105664860987)
XLA Ops:
  6.5 1.8 fusion.155
  9.8 8.3 %compare_and_fusion = (pred[384]{0:T(512)(128)(4,1)S(1)}, pred[384]{0:T(512)(128)(4,1)S(1)}) fusion(s32[3,128]{1,0:T(4,128)} %constant.273.clone.1, s32[3]{0:T(128)S(1)} %iota_multiply_fusion, s32[]{:T(128)} %bitcast.16, s32[]{:T(128)} %bitcast.15, s32[384]{0:T(512)S(1)} %fusion.148, s32[]{:T(128)} %bitcast.14, s32[]{:T(128)} %bitcast.13, s32[]{:T(128)} %bitcast.12, ...), kind=kLoop, calls=%fused_computation.165 | loop fusion | flops 14592 | bytes 3900 | tf_op jit(solution)/shard_map/jit(_take)/and | solution.py:35
  19.0 1.8 gather_fusion
  23.9 4.2 %all-to-all-start = ((bf16[2,2,13312]{2,1,0:T(2,128)(2,1)}), bf16[2,2,13312]{2,1,0:T(2,128)(2,1)S(1)}, u32[]{:S(2)}, u32[]{:S(2)}) async-start(bf16[2,2,13312]{2,1,0:T(2,128)(2,1)} %reshape.390), calls=%async_computation | async-start | bytes 212992 | tf_op jit(solution)/shard_map/all_to_all | solution.py:120
  30.5 14.0 %all_gather.15 = f32[16,4,24]{2,1,0:T(4,128)S(1)} all-gather(f32[4,4,24]{2,1,0:T(4,128)S(1)} %constant_dynamic-slice_fusion.1), channel_id=1, replica_groups=mesh['pixel'=4,'crop'=2,'member'=4] {'member'}, dimensions={0}, use_global_device_ids=true | all-gather | bytes 7680 | tf_op jit(solution)/shard_map/all_gather | solution.py:181
  49.3 3.5 all-to-all-start.1
  54.3 4.6 %all-to-all-done.1 = bf16[2,2,53248]{2,1,0:T(2,128)(2,1)S(1)} async-done(((bf16[2,2,53248]{2,1,0:T(2,128)(2,1)}), bf16[2,2,53248]{2,1,0:T(2,128)(2,1)S(1)}, u32[]{:S(2)}, u32[]{:S(2)}) %all-to-all-start.1) | async-done | bytes 426016 | tf_op jit(solution)/shard_map/all_to_all | solution.py:119
  61.1 177.1 %while.14 = (s32[]{:T(128)}, f32[4,52,4,128]{3,2,1,0:T(4,128)}, bf16[4,48,32]{1,2,0:T(8,128)(2,1)}, bf16[52,8,4,128]{3,1,0,2:T(8,128)(2,1)S(1)}, bf16[4,8,24]{2,...) while((s32[]{:T(128)}, f32[4,52,4,128]{3,2,1,0:T(4,128)}, ...), condition=%wide.region_3.4_spmd.clone, body=%wide.region_1.3_spmd.clone.sunk | while | flops 1153157120 | bytes 92354224 | solution.py:143
  64.0 3.1 fusion.222
  67.1 1.9 slice.223
  69.0 6.3 %fusion.223 = bf16[52,48,4,128]{3,1,0,2:T(8,128)(2,1)} fusion(bf16[52,48,4,128]{3,1,0,2:T(8,128)(2,1)S(1)} %fusion.221, f32[4,52,128,48]{2,3,1,0:T(8,128)} %fusion.222, bf16[51,48,4,128]{3,1,0,2:T(8,128)(2,1)} %slice.223, bf16[4,3,48,48]{3,2,0,1:T(8,128)(2,1)} %get-tuple-element.289, bf16[4,3,48,96]{3,2,0,1:T(8,128)(2,1)S(1)} %get-tuple-element.288), kind=kOutput, calls=%fused_computation.7.clone.1 | convolution fusion | flops 253034496 | bytes 12828672 | tf_op jit(solution)/shard_map/while/body/eval_jaxpr/koc,tckq->tokq/dot_general | solution.py:86
  75.3 4.8 %fusion.224 = f32[4,52,128,48]{2,3,1,0:T(8,128)} fusion(bf16[52,48,4,128]{3,1,0,2:T(8,128)(2,1)} %fusion.223, bf16[4,3,48,96]{3,2,0,1:T(8,128)(2,1)S(1)} %get-tuple-element.288), kind=kOutput, calls=%fused_computation.38.clone.1 | convolution fusion | flops 122683392 | bytes 7716864 | tf_op jit(solution)/shard_map/while/body/eval_jaxpr/koc,tckq->tokq/dot_general | solution.py:73
  81.8 6.3 %fusion.225 = bf16[52,48,4,128]{3,1,0,2:T(8,128)(2,1)} fusion(bf16[52,48,4,128]{3,1,0,2:T(8,128)(2,1)} %fusion.223, f32[4,52,128,48]{2,3,1,0:T(8,128)} %fusion.224, bf16[50,48,4,128]{3,1,0,2:T(8,128)(2,1)S(1)} %slice-done, bf16[4,3,48,48]{3,2,0,1:T(8,128)(2,1)} %get-tuple-element.289, bf16[4,3,48,96]{3,2,0,1:T(8,128)(2,1)S(1)} %get-tuple-element.288), kind=kOutput, calls=%fused_computation.5.clone.1 | convolution fusion | flops 253034496 | bytes 12779520 | tf_op jit(solution)/shard_map/while/body/eval_jaxpr/koc,tckq->tokq/dot_general | solution.py:86
  88.1 4.8 %fusion.226 = f32[4,52,128,48]{2,3,1,0:T(8,128)} fusion(bf16[52,48,4,128]{3,1,0,2:T(8,128)(2,1)} %fusion.225, bf16[4,3,48,96]{3,2,0,1:T(8,128)(2,1)S(1)} %get-tuple-element.288), kind=kOutput, calls=%fused_computation.34.clone.1 | convolution fusion | flops 122683392 | bytes 7716864 | tf_op jit(solution)/shard_map/while/body/eval_jaxpr/koc,tckq->tokq/dot_general | solution.py:73
  94.6 6.3 %fusion.227 = f32[4,52,128,48]{2,3,1,0:T(8,128)} fusion(f32[4,52,128,48]{2,3,1,0:T(8,128)} %fusion.226, bf16[48,48,4,128]{3,1,0,2:T(8,128)(2,1)S(1)} %slice-done.1, bf16[4,3,48,48]{3,2,0,1:T(8,128)(2,1)} %get-tuple-element.289, bf16[4,3,48,96]{3,2,0,1:T(8,128)(2,1)S(1)} %get-tuple-element.288), kind=kOutput, calls=%fused_computation.18.clone.1 | convolution fusion | flops 249200640 | bytes 12681216 | tf_op jit(solution)/shard_map/while/body/eval_jaxpr/koc,tckq->tokq/dot_general | solution.py:86
  100.9 3.8 %fusion.228 = f32[4,1,52,128]{3,1,2,0:T(1,128)S(1)} fusion(f32[4,52,128,48]{2,3,1,0:T(8,128)} %fusion.227, bf16[52,48,4,128]{3,1,0,2:T(8,128)(2,1)} %fusion.225, bf16[4,48,1,1]{1,0,2,3:T(4,128)(2,1)S(1)} %bitcast.293), kind=kOutput, calls=%fused_computation.19.clone.1 | convolution fusion | flops 6389760 | bytes 7774592 | tf_op jit(solution)/shard_map/while/body/eval_jaxpr/kc,tckq->tkq/dot_general | solution.py:90
  108.3 3.1 fusion.222
  111.3 1.9 slice.223
  113.3 6.3 %fusion.223 = bf16[52,48,4,128]{3,1,0,2:T(8,128)(2,1)} fusion(bf16[52,48,4,128]{3,1,0,2:T(8,128)(2,1)S(1)} %fusion.221, f32[4,52,128,48]{2,3,1,0:T(8,128)} %fusion.222, bf16[51,48,4,128]{3,1,0,2:T(8,128)(2,1)} %slice.223, bf16[4,3,48,48]{3,2,0,1:T(8,128)(2,1)} %get-tuple-element.289, bf16[4,3,48,96]{3,2,0,1:T(8,128)(2,1)S(1)} %get-tuple-element.288), kind=kOutput, calls=%fused_computation.7.clone.1 | convolution fusion | flops 253034496 | bytes 12828672 | tf_op jit(solution)/shard_map/while/body/eval_jaxpr/koc,tckq->tokq/dot_general | solution.py:86
  119.5 4.8 %fusion.224 = f32[4,52,128,48]{2,3,1,0:T(8,128)} fusion(bf16[52,48,4,128]{3,1,0,2:T(8,128)(2,1)} %fusion.223, bf16[4,3,48,96]{3,2,0,1:T(8,128)(2,1)S(1)} %get-tuple-element.288), kind=kOutput, calls=%fused_computation.38.clone.1 | convolution fusion | flops 122683392 | bytes 7716864 | tf_op jit(solution)/shard_map/while/body/eval_jaxpr/koc,tckq->tokq/dot_general | solution.py:73
  124.3 1.7 slice-done
  126.0 6.3 %fusion.225 = bf16[52,48,4,128]{3,1,0,2:T(8,128)(2,1)} fusion(bf16[52,48,4,128]{3,1,0,2:T(8,128)(2,1)} %fusion.223, f32[4,52,128,48]{2,3,1,0:T(8,128)} %fusion.224, bf16[50,48,4,128]{3,1,0,2:T(8,128)(2,1)S(1)} %slice-done, bf16[4,3,48,48]{3,2,0,1:T(8,128)(2,1)} %get-tuple-element.289, bf16[4,3,48,96]{3,2,0,1:T(8,128)(2,1)S(1)} %get-tuple-element.288), kind=kOutput, calls=%fused_computation.5.clone.1 | convolution fusion | flops 253034496 | bytes 12779520 | tf_op jit(solution)/shard_map/while/body/eval_jaxpr/koc,tckq->tokq/dot_general | solution.py:86
  132.3 4.8 %fusion.226 = f32[4,52,128,48]{2,3,1,0:T(8,128)} fusion(bf16[52,48,4,128]{3,1,0,2:T(8,128)(2,1)} %fusion.225, bf16[4,3,48,96]{3,2,0,1:T(8,128)(2,1)S(1)} %get-tuple-element.288), kind=kOutput, calls=%fused_computation.34.clone.1 | convolution fusion | flops 122683392 | bytes 7716864 | tf_op jit(solution)/shard_map/while/body/eval_jaxpr/koc,tckq->tokq/dot_general | solution.py:73
  138.8 6.3 %fusion.227 = f32[4,52,128,48]{2,3,1,0:T(8,128)} fusion(f32[4,52,128,48]{2,3,1,0:T(8,128)} %fusion.226, bf16[48,48,4,128]{3,1,0,2:T(8,128)(2,1)S(1)} %slice-done.1, bf16[4,3,48,48]{3,2,0,1:T(8,128)(2,1)} %get-tuple-element.289, bf16[4,3,48,96]{3,2,0,1:T(8,128)(2,1)S(1)} %get-tuple-element.288), kind=kOutput, calls=%fused_computation.18.clone.1 | convolution fusion | flops 249200640 | bytes 12681216 | tf_op jit(solution)/shard_map/while/body/eval_jaxpr/koc,tckq->tokq/dot_general | solution.py:86
  145.1 3.8 %fusion.228 = f32[4,1,52,128]{3,1,2,0:T(1,128)S(1)} fusion(f32[4,52,128,48]{2,3,1,0:T(8,128)} %fusion.227, bf16[52,48,4,128]{3,1,0,2:T(8,128)(2,1)} %fusion.225, bf16[4,48,1,1]{1,0,2,3:T(4,128)(2,1)S(1)} %bitcast.293), kind=kOutput, calls=%fused_computation.19.clone.1 | convolution fusion | flops 6389760 | bytes 7774592 | tf_op jit(solution)/shard_map/while/body/eval_jaxpr/kc,tckq->tkq/dot_general | solution.py:90
  152.5 3.1 fusion.222
  155.6 1.9 slice.223
  157.5 6.3 %fusion.223 = bf16[52,48,4,128]{3,1,0,2:T(8,128)(2,1)} fusion(bf16[52,48,4,128]{3,1,0,2:T(8,128)(2,1)S(1)} %fusion.221, f32[4,52,128,48]{2,3,1,0:T(8,128)} %fusion.222, bf16[51,48,4,128]{3,1,0,2:T(8,128)(2,1)} %slice.223, bf16[4,3,48,48]{3,2,0,1:T(8,128)(2,1)} %get-tuple-element.289, bf16[4,3,48,96]{3,2,0,1:T(8,128)(2,1)S(1)} %get-tuple-element.288), kind=kOutput, calls=%fused_computation.7.clone.1 | convolution fusion | flops 253034496 | bytes 12828672 | tf_op jit(solution)/shard_map/while/body/eval_jaxpr/koc,tckq->tokq/dot_general | solution.py:86
  163.8 4.8 %fusion.224 = f32[4,52,128,48]{2,3,1,0:T(8,128)} fusion(bf16[52,48,4,128]{3,1,0,2:T(8,128)(2,1)} %fusion.223, bf16[4,3,48,96]{3,2,0,1:T(8,128)(2,1)S(1)} %get-tuple-element.288), kind=kOutput, calls=%fused_computation.38.clone.1 | convolution fusion | flops 122683392 | bytes 7716864 | tf_op jit(solution)/shard_map/while/body/eval_jaxpr/koc,tckq->tokq/dot_general | solution.py:73
  170.3 6.3 %fusion.225 = bf16[52,48,4,128]{3,1,0,2:T(8,128)(2,1)} fusion(bf16[52,48,4,128]{3,1,0,2:T(8,128)(2,1)} %fusion.223, f32[4,52,128,48]{2,3,1,0:T(8,128)} %fusion.224, bf16[50,48,4,128]{3,1,0,2:T(8,128)(2,1)S(1)} %slice-done, bf16[4,3,48,48]{3,2,0,1:T(8,128)(2,1)} %get-tuple-element.289, bf16[4,3,48,96]{3,2,0,1:T(8,128)(2,1)S(1)} %get-tuple-element.288), kind=kOutput, calls=%fused_computation.5.clone.1 | convolution fusion | flops 253034496 | bytes 12779520 | tf_op jit(solution)/shard_map/while/body/eval_jaxpr/koc,tckq->tokq/dot_general | solution.py:86
  176.6 4.8 %fusion.226 = f32[4,52,128,48]{2,3,1,0:T(8,128)} fusion(bf16[52,48,4,128]{3,1,0,2:T(8,128)(2,1)} %fusion.225, bf16[4,3,48,96]{3,2,0,1:T(8,128)(2,1)S(1)} %get-tuple-element.288), kind=kOutput, calls=%fused_computation.34.clone.1 | convolution fusion | flops 122683392 | bytes 7716864 | tf_op jit(solution)/shard_map/while/body/eval_jaxpr/koc,tckq->tokq/dot_general | solution.py:73
  183.1 6.3 %fusion.227 = f32[4,52,128,48]{2,3,1,0:T(8,128)} fusion(f32[4,52,128,48]{2,3,1,0:T(8,128)} %fusion.226, bf16[48,48,4,128]{3,1,0,2:T(8,128)(2,1)S(1)} %slice-done.1, bf16[4,3,48,48]{3,2,0,1:T(8,128)(2,1)} %get-tuple-element.289, bf16[4,3,48,96]{3,2,0,1:T(8,128)(2,1)S(1)} %get-tuple-element.288), kind=kOutput, calls=%fused_computation.18.clone.1 | convolution fusion | flops 249200640 | bytes 12681216 | tf_op jit(solution)/shard_map/while/body/eval_jaxpr/koc,tckq->tokq/dot_general | solution.py:86
  189.4 3.8 %fusion.228 = f32[4,1,52,128]{3,1,2,0:T(1,128)S(1)} fusion(f32[4,52,128,48]{2,3,1,0:T(8,128)} %fusion.227, bf16[52,48,4,128]{3,1,0,2:T(8,128)(2,1)} %fusion.225, bf16[4,48,1,1]{1,0,2,3:T(4,128)(2,1)S(1)} %bitcast.293), kind=kOutput, calls=%fused_computation.19.clone.1 | convolution fusion | flops 6389760 | bytes 7774592 | tf_op jit(solution)/shard_map/while/body/eval_jaxpr/kc,tckq->tkq/dot_general | solution.py:90
  196.8 3.1 fusion.222
  199.9 1.9 slice.223
  201.8 6.3 %fusion.223 = bf16[52,48,4,128]{3,1,0,2:T(8,128)(2,1)} fusion(bf16[52,48,4,128]{3,1,0,2:T(8,128)(2,1)S(1)} %fusion.221, f32[4,52,128,48]{2,3,1,0:T(8,128)} %fusion.222, bf16[51,48,4,128]{3,1,0,2:T(8,128)(2,1)} %slice.223, bf16[4,3,48,48]{3,2,0,1:T(8,128)(2,1)} %get-tuple-element.289, bf16[4,3,48,96]{3,2,0,1:T(8,128)(2,1)S(1)} %get-tuple-element.288), kind=kOutput, calls=%fused_computation.7.clone.1 | convolution fusion | flops 253034496 | bytes 12828672 | tf_op jit(solution)/shard_map/while/body/eval_jaxpr/koc,tckq->tokq/dot_general | solution.py:86
  208.1 4.8 %fusion.224 = f32[4,52,128,48]{2,3,1,0:T(8,128)} fusion(bf16[52,48,4,128]{3,1,0,2:T(8,128)(2,1)} %fusion.223, bf16[4,3,48,96]{3,2,0,1:T(8,128)(2,1)S(1)} %get-tuple-element.288), kind=kOutput, calls=%fused_computation.38.clone.1 | convolution fusion | flops 122683392 | bytes 7716864 | tf_op jit(solution)/shard_map/while/body/eval_jaxpr/koc,tckq->tokq/dot_general | solution.py:73
  214.5 6.3 %fusion.225 = bf16[52,48,4,128]{3,1,0,2:T(8,128)(2,1)} fusion(bf16[52,48,4,128]{3,1,0,2:T(8,128)(2,1)} %fusion.223, f32[4,52,128,48]{2,3,1,0:T(8,128)} %fusion.224, bf16[50,48,4,128]{3,1,0,2:T(8,128)(2,1)S(1)} %slice-done, bf16[4,3,48,48]{3,2,0,1:T(8,128)(2,1)} %get-tuple-element.289, bf16[4,3,48,96]{3,2,0,1:T(8,128)(2,1)S(1)} %get-tuple-element.288), kind=kOutput, calls=%fused_computation.5.clone.1 | convolution fusion | flops 253034496 | bytes 12779520 | tf_op jit(solution)/shard_map/while/body/eval_jaxpr/koc,tckq->tokq/dot_general | solution.py:86
  220.9 4.8 %fusion.226 = f32[4,52,128,48]{2,3,1,0:T(8,128)} fusion(bf16[52,48,4,128]{3,1,0,2:T(8,128)(2,1)} %fusion.225, bf16[4,3,48,96]{3,2,0,1:T(8,128)(2,1)S(1)} %get-tuple-element.288), kind=kOutput, calls=%fused_computation.34.clone.1 | convolution fusion | flops 122683392 | bytes 7716864 | tf_op jit(solution)/shard_map/while/body/eval_jaxpr/koc,tckq->tokq/dot_general | solution.py:73
  227.4 6.3 %fusion.227 = f32[4,52,128,48]{2,3,1,0:T(8,128)} fusion(f32[4,52,128,48]{2,3,1,0:T(8,128)} %fusion.226, bf16[48,48,4,128]{3,1,0,2:T(8,128)(2,1)S(1)} %slice-done.1, bf16[4,3,48,48]{3,2,0,1:T(8,128)(2,1)} %get-tuple-element.289, bf16[4,3,48,96]{3,2,0,1:T(8,128)(2,1)S(1)} %get-tuple-element.288), kind=kOutput, calls=%fused_computation.18.clone.1 | convolution fusion | flops 249200640 | bytes 12681216 | tf_op jit(solution)/shard_map/while/body/eval_jaxpr/koc,tckq->tokq/dot_general | solution.py:86
  233.7 3.8 %fusion.228 = f32[4,1,52,128]{3,1,2,0:T(1,128)S(1)} fusion(f32[4,52,128,48]{2,3,1,0:T(8,128)} %fusion.227, bf16[52,48,4,128]{3,1,0,2:T(8,128)(2,1)} %fusion.225, bf16[4,48,1,1]{1,0,2,3:T(4,128)(2,1)S(1)} %bitcast.293), kind=kOutput, calls=%fused_computation.19.clone.1 | convolution fusion | flops 6389760 | bytes 7774592 | tf_op jit(solution)/shard_map/while/body/eval_jaxpr/kc,tckq->tkq/dot_general | solution.py:90
  241.2 33.1 %all-reduce.6.cloned.1.call-done = f32[52,512]{1,0:T(8,128)} async-done(((f32[52,512]{1,0:T(8,128)}), f32[52,512]{1,0:T(8,128)}) %all-reduce.6.cloned.1.call-update) | async-done | bytes 106512 | tf_op jit(solution)/shard_map/psum | solution.py:145
  275.8 19.9 %all_gather.12 = bf16[16,52,512]{2,1,0:T(8,128)(2,1)S(1)} all-gather(bf16[4,52,512]{2,1,0:T(8,128)(2,1)S(1)} %copy.170), channel_id=1, replica_groups=mesh['pixel'=4,'crop'=2,'member'=4] {'member'}, dimensions={0}, use_global_device_ids=true | all-gather | bytes 1064960 | tf_op jit(solution)/shard_map/all_gather | solution.py:160
  297.3 23.8 %all-reduce.3 = (f32[8,4,16]{2,0,1:T(8,128)S(1)}, f32[8,4]{1,0:T(8,128)S(1)}) all-reduce(f32[8,4,16]{2,0,1:T(8,128)S(1)} %fusion.94, f32[8,4]{1,0:T(8,128)S(1)} %convolution_bitcast_fusion.2), channel_id=1, replica_groups=mesh['pixel'=4,'crop'=2,'member'=4] {'pixel','crop'}, use_global_device_ids=true, to_apply=%region_6.7 | all-reduce | flops 544 | bytes 4352 | tf_op jit(solution)/shard_map/psum | solution.py:174
  321.2 13.1 %all_gather.13 = f32[4,16,16]{2,0,1:T(4,128)S(1)} all-gather(f32[4,4,16]{2,0,1:T(4,128)S(1)} %constant_dynamic-slice_fusion), channel_id=1, replica_groups=mesh['pixel'=4,'crop'=2,'member'=4] {'member'}, dimensions={1}, use_global_device_ids=true | all-gather | bytes 5120 | tf_op jit(solution)/shard_map/all_gather | solution.py:179
  334.5 5.9 %custom-call.11 = f32[4,16,16]{2,1,0:T(8,128)S(1)} custom-call(f32[4,16,16]{2,1,0:T(8,128)S(1)} %fusion.130), custom_call_target="Cholesky" | custom-call | tf_op jit(solution)/shard_map/vmap(jit(cholesky))/cholesky | solution.py:188
  340.6 4.9 %custom-call.12 = f32[4,1,16,16]{2,3,1,0:T(8,128)S(1)} custom-call(f32[4,1,16,16]{3,2,1,0:T(8,128)S(1)} %select_bitcast_fusion), custom_call_target="InvertDiagBlocksLowerTriangular" | custom-call | tf_op jit(solution)/shard_map/vmap(jit(_cho_solve))/triangular_solve | solution.py:191
  345.6 11.9 %all-gather = f32[4,4,4]{2,1,0:T(4,128)S(1)} all-gather(f32[1,4,4]{2,1,0:T(4,128)S(1)} %bitcast.296), channel_id=1, replica_groups=mesh['pixel'=4,'crop'=2,'member'=4] {'member'}, dimensions={0}, use_global_device_ids=true | all-gather | bytes 320 | tf_op jit(solution)/shard_map/all_gather | solution.py:180
  (176 shorter events, 50.6 us)
Async XLA Ops:
  6.5 22.7 %copy-start = (bf16[52,8,384]{2,1,0:T(8,128)(2,1)S(1)}, bf16[52,8,384]{2,1,0:T(8,128)(2,1)}, u32[]{:S(2)}) copy-start(bf16[52,8,384]{2,1,0:T(8,128)(2,1)} %param.17) | copy-start | bytes 958468
  19.0 11.4 %copy-start.10 = (f32[4,8,24]{2,1,0:T(8,128)S(1)}, f32[4,8,24]{2,1,0:T(8,128)}, u32[]{:S(2)}) copy-start(f32[4,8,24]{2,1,0:T(8,128)} %param.23) | copy-start | bytes 9220
  23.9 25.4 %all-to-all-start = ((bf16[2,2,13312]{2,1,0:T(2,128)(2,1)}), bf16[2,2,13312]{2,1,0:T(2,128)(2,1)S(1)}, u32[]{:S(2)}, u32[]{:S(2)}) async-start(bf16[2,2,13312]{2,1,0:T(2,128)(2,1)} %reshape.390), calls=%async_computation | async-start | bytes 212992 | tf_op jit(solution)/shard_map/all_to_all | solution.py:120
  29.8 17.6 %copy-start.1 = (bf16[4,3,48,96]{3,2,1,0:T(8,128)(2,1)S(1)}, bf16[4,3,48,96]{3,2,1,0:T(8,128)(2,1)}, u32[]{:S(2)}) copy-start(bf16[4,3,48,96]{3,2,1,0:T(8,128)(2,1)} %param.25) | copy-start | bytes 331780
  29.8 17.6 %copy-start.2 = (bf16[4,3,48,48]{3,2,1,0:T(8,128)(2,1)S(1)}, bf16[4,3,48,48]{3,2,1,0:T(8,128)(2,1)}, u32[]{:S(2)}) copy-start(bf16[4,3,48,48]{3,2,1,0:T(8,128)(2,1)} %param.26) | copy-start | bytes 165892
  30.5 14.7 %copy-start.5 = (f32[4,4,24]{2,1,0:T(4,128)}, f32[4,4,24]{2,1,0:T(4,128)S(1)}, u32[]{:S(2)}) copy-start(f32[4,4,24]{2,1,0:T(4,128)S(1)} %constant_dynamic-slice_fusion.1) | copy-start | bytes 4612
  49.3 9.5 %all-to-all-start.1 = ((bf16[2,2,53248]{2,1,0:T(2,128)(2,1)}), bf16[2,2,53248]{2,1,0:T(2,128)(2,1)S(1)}, u32[]{:S(2)}, u32[]{:S(2)}) async-start(bf16[2,2,53248]{2,1,0:T(2,128)(2,1)} %reshape.388), calls=%async_computation.1 | async-start | bytes 851968 | tf_op jit(solution)/shard_map/all_to_all | solution.py:119
  52.8 221.5 %all-reduce.6.cloned.1.call-start = ((), (), s32[]{:S(2)}) async-start(), calls=%async_computation.2 | async-start | bytes 229376 | tf_op jit(solution)/shard_map/psum | solution.py:145
  61.1 1.3 copy-start.8
  61.1 1.3 copy-start.11
  80.1 1.7 slice-start
  92.9 1.7 slice-start.1
  94.6 6.3 %copy-start.4 = (bf16[4,48]{1,0:T(4,128)(2,1)S(1)}, bf16[4,48]{1,0:T(4,128)(2,1)}, u32[]{:S(2)}) copy-start(bf16[4,48]{1,0:T(4,128)(2,1)} %get-tuple-element.290) | copy-start | bytes 1156 | tf_op jit(solution)/shard_map/while
  100.9 4.5 %copy-start.9 = (bf16[4,8,24]{2,1,0:T(8,128)(2,1)S(1)}, bf16[4,8,24]{2,1,0:T(8,128)(2,1)}, u32[]{:S(2)}) copy-start(bf16[4,8,24]{2,1,0:T(8,128)(2,1)} %copy-done.8) | copy-start | bytes 4612 | tf_op jit(solution)/shard_map/while
  100.9 4.5 %copy-start.12 = (s32[128]{0:T(128)S(1)}, s32[128]{0:T(128)}, u32[]{:S(2)}) copy-start(s32[128]{0:T(128)} %copy-done.11) | copy-start | bytes 1540 | tf_op jit(solution)/shard_map/while
  105.4 1.3 copy-start.8
  105.4 1.3 copy-start.11
  124.3 1.7 slice-start
  137.2 1.7 slice-start.1
  138.8 6.3 %copy-start.4 = (bf16[4,48]{1,0:T(4,128)(2,1)S(1)}, bf16[4,48]{1,0:T(4,128)(2,1)}, u32[]{:S(2)}) copy-start(bf16[4,48]{1,0:T(4,128)(2,1)} %get-tuple-element.290) | copy-start | bytes 1156 | tf_op jit(solution)/shard_map/while
  145.1 4.5 %copy-start.9 = (bf16[4,8,24]{2,1,0:T(8,128)(2,1)S(1)}, bf16[4,8,24]{2,1,0:T(8,128)(2,1)}, u32[]{:S(2)}) copy-start(bf16[4,8,24]{2,1,0:T(8,128)(2,1)} %copy-done.8) | copy-start | bytes 4612 | tf_op jit(solution)/shard_map/while
  145.1 4.5 %copy-start.12 = (s32[128]{0:T(128)S(1)}, s32[128]{0:T(128)}, u32[]{:S(2)}) copy-start(s32[128]{0:T(128)} %copy-done.11) | copy-start | bytes 1540 | tf_op jit(solution)/shard_map/while
  149.6 1.3 copy-start.8
  149.6 1.3 copy-start.11
  168.6 1.7 slice-start
  181.4 1.7 slice-start.1
  183.1 6.3 %copy-start.4 = (bf16[4,48]{1,0:T(4,128)(2,1)S(1)}, bf16[4,48]{1,0:T(4,128)(2,1)}, u32[]{:S(2)}) copy-start(bf16[4,48]{1,0:T(4,128)(2,1)} %get-tuple-element.290) | copy-start | bytes 1156 | tf_op jit(solution)/shard_map/while
  189.4 4.5 %copy-start.9 = (bf16[4,8,24]{2,1,0:T(8,128)(2,1)S(1)}, bf16[4,8,24]{2,1,0:T(8,128)(2,1)}, u32[]{:S(2)}) copy-start(bf16[4,8,24]{2,1,0:T(8,128)(2,1)} %copy-done.8) | copy-start | bytes 4612 | tf_op jit(solution)/shard_map/while
  189.4 4.5 %copy-start.12 = (s32[128]{0:T(128)S(1)}, s32[128]{0:T(128)}, u32[]{:S(2)}) copy-start(s32[128]{0:T(128)} %copy-done.11) | copy-start | bytes 1540 | tf_op jit(solution)/shard_map/while
  193.9 1.3 copy-start.8
  193.9 1.3 copy-start.11
  212.9 1.7 slice-start
  225.7 1.7 slice-start.1
  227.4 6.3 %copy-start.4 = (bf16[4,48]{1,0:T(4,128)(2,1)S(1)}, bf16[4,48]{1,0:T(4,128)(2,1)}, u32[]{:S(2)}) copy-start(bf16[4,48]{1,0:T(4,128)(2,1)} %get-tuple-element.290) | copy-start | bytes 1156 | tf_op jit(solution)/shard_map/while
  233.7 4.5 %copy-start.9 = (bf16[4,8,24]{2,1,0:T(8,128)(2,1)S(1)}, bf16[4,8,24]{2,1,0:T(8,128)(2,1)}, u32[]{:S(2)}) copy-start(bf16[4,8,24]{2,1,0:T(8,128)(2,1)} %copy-done.8) | copy-start | bytes 4612 | tf_op jit(solution)/shard_map/while
  233.7 4.5 %copy-start.12 = (s32[128]{0:T(128)S(1)}, s32[128]{0:T(128)}, u32[]{:S(2)}) copy-start(s32[128]{0:T(128)} %copy-done.11) | copy-start | bytes 1540 | tf_op jit(solution)/shard_map/while
  238.2 57.5 %copy-start.15 = (pred[8,512]{1,0:T(8,128)(4,1)S(1)}, pred[8,512]{1,0:T(8,128)(4,1)}, u32[]{:S(2)}) copy-start(pred[8,512]{1,0:T(8,128)(4,1)} %iota_compare_fusion.3) | copy-start | bytes 12292
  295.6 38.7 %copy-start.7 = (f32[16,16]{0,1:T(8,128)S(1)}, f32[16,16]{0,1:T(8,128)}, u32[]{:S(2)}) copy-start(f32[16,16]{0,1:T(8,128)} %copy.173) | copy-start | bytes 3076
  295.6 44.7 %copy-start.14 = (pred[16,16]{1,0:T(8,128)(4,1)S(1)}, pred[16,16]{1,0:T(8,128)(4,1)}, u32[]{:S(2)}) copy-start(pred[16,16]{1,0:T(8,128)(4,1)} %iota_compare_fusion.4) | copy-start | bytes 772
  295.6 44.9 %copy-start.13 = (pred[16,16]{1,0:T(8,128)(4,1)S(1)}, pred[16,16]{1,0:T(8,128)(4,1)}, u32[]{:S(2)}) copy-start(pred[16,16]{1,0:T(8,128)(4,1)} %iota_compare_fusion.5) | copy-start | bytes 772
  295.6 62.8 %copy-start.3 = (f32[4,16,24]{2,0,1:T(4,128)S(1)}, f32[4,16,24]{2,0,1:T(4,128)}, u32[]{:S(2)}) copy-start(f32[4,16,24]{2,0,1:T(4,128)} %multiply_bitcast_fusion) | copy-start | bytes 18436
  295.7 62.8 %copy-start.6 = (f32[4,4,24]{2,1,0:T(4,128)S(1)}, f32[4,4,24]{2,1,0:T(4,128)}, u32[]{:S(2)}) copy-start(f32[4,4,24]{2,1,0:T(4,128)} %copy-done.5) | copy-start | bytes 4612
Sparse Core Ops, SparseCore 0:
  240.1 34.1 all-reduce.5
where the time goes:
time: 368 us; the launch traced here: 366 us
  matrix products  156 us (42%)
  blocking collectives  82.7 us (22%)
  local copies, waits for them, and re-layouts  39 us (11%)
  waiting for transfers between devices  37.7 us (10%)
  other arithmetic  29.4 us (8%)
  between operations  13.7 us (4%)
  starting transfers between devices  7.72 us (2%)
    dot_general x12, matrix products, run_network(): jnp.einsum('koc,tckq->tokq', mix_weight[:, layer], inner, preferred_eleme...  75.5 us
    dot_general x12, matrix products, run_network(): jnp.einsum('koc,tckq->tokq', conv_weight[:, layer, :, :n_channels], hidde...  50.8 us
    psum x1, waiting for transfers between devices, local(): mean_pred = lax.psum(jnp.sum(predicted, axis=0), 'member') / members  33.1 us
    psum x1, blocking collectives, local(): gram_sum, proj_sum = lax.psum((gram_rows, proj_rows), ('pixel', 'crop'))  23.8 us
    slice x20, local copies, waits for them, and re-layouts, run_network(): hidden[:n_weeks - dilation]  21.1 us
    all_gather x1, blocking collectives, local(): shard_rows = lax.all_gather(scaled, 'member', axis=0, tiled=True)  19.9 us
    dot_general x4, matrix products, run_network(): jnp.einsum('kc,tckq->tkq', head_weight, hidden, preferred_element_type=jn...  15.2 us
    all_gather x1, blocking collectives, local(): lax.all_gather(theta_mine, 'member', axis=0, tiled=True)  14 us
  transfers between devices with their start and end apart: 3, of which 2 were waited for; matrix products, arithmetic and copies ran while one was open for 3% of the time, Pallas kernels for 0%

commit v1 on v0

v1 whole, which is shorter than its diff:
```python
import functools
import math

import jax
import jax.numpy as jnp
from jax import lax
from jax.experimental import pallas as pl
from jax.experimental.pallas import tpu as pltpu
from jax.sharding import PartitionSpec as P

REGIONS = 8
CAP = 8
SLOTS = REGIONS * CAP
LANES = 2 * SLOTS
ALPHA_INFLATION = 4.0
VMEM_LIMIT = 48 * 2**20
F32 = jnp.float32
BF16 = jnp.bfloat16

NT = (((1,), (1,)), ((), ()))
TN = (((0,), (0,)), ((), ()))


def mm(a, b):
    return jnp.dot(a, b, preferred_element_type=F32)


def mm_nt(a, b):
    return lax.dot_general(a, b, NT, preferred_element_type=F32)


def hi_lo(x):
    high = x.astype(BF16)
    return high, (x - high.astype(F32)).astype(BF16)


def vmem(n):
    return [pl.BlockSpec(memory_space=pltpu.VMEM)] * n


def hbm(n):
    return [pl.BlockSpec(memory_space=pltpu.HBM)] * n


def stay(*arrays):
    return [pltpu.with_memory_space_constraint(a, pltpu.HBM) for a in arrays]


def weight_rows(layers, channels):
    taps = layers * channels
    return taps, taps + 16


def fetch(pairs, sems):
    copies = [pltpu.make_async_copy(src, dst, sems.at[i]) for i, (src, dst) in enumerate(pairs)]
    for copy in copies:
        copy.start()

    def wait():
        for copy in copies:
            copy.wait()

    return wait


def fold_weights(
    split, input_hbm, conv_hbm, mix_hbm, head_hbm, theta_hbm, out_ref, theta_ref,
    input_ref, conv_ref, mix_ref, head_ref, quad, stack, sems,
):
    layers, channels = conv_ref.shape[0], conv_ref.shape[1]
    forcing = 8
    mine = lax.axis_index("member") // split
    wait = fetch(
        [
            (input_hbm.at[mine], input_ref),
            (conv_hbm.at[mine], conv_ref),
            (mix_hbm.at[mine], mix_ref),
            (head_hbm, head_ref),
            (theta_hbm, theta_ref),
        ],
        sems,
    )
    taps, block = weight_rows(layers, channels)
    out_ref[...] = jnp.zeros(out_ref.shape, BF16)
    quad[...] = jnp.zeros(quad.shape, F32)
    stack[...] = jnp.zeros(stack.shape, F32)
    wait()
    win = jnp.transpose(input_ref[...].astype(F32))
    for half in range(2):
        rows = pl.ds(half * channels, channels)
        quad[rows, pl.ds(half * forcing, forcing)] = win[:, :forcing]
        for layer in range(layers - 1):
            at = 2 * forcing + (2 * layer + half) * channels
            quad[rows, pl.ds(at, channels)] = mix_ref[layer].astype(F32)
    for layer in range(layers):
        stack[pl.ds(layer * channels, channels), pl.ds(0, 2 * channels)] = conv_ref[layer].astype(
            F32
        )
    head_row = lax.broadcasted_iota(jnp.int32, head_ref.shape, 0)
    head = jnp.sum(
        jnp.where(head_row == mine, head_ref[...].astype(F32), 0.0), axis=0, keepdims=True
    )
    stack[pl.ds(taps, 1), pl.ds(0, channels)] = head
    lhs = stack[:, : 2 * channels].astype(BF16)
    fused = mm(lhs, quad[...].astype(BF16))
    last = mm(lhs[taps:, :channels], mix_ref[layers - 1])
    width = fused.shape[1]
    out_ref[pl.ds(0, taps), pl.ds(0, width)] = fused[:taps].astype(BF16)
    fused_hi, fused_lo = hi_lo(fused[taps : taps + 1])
    last_hi, last_lo = hi_lo(last[:1])
    last_pad = jnp.zeros((2, width - channels), F32)
    last_rows = jnp.concatenate([last_hi.astype(F32), last_lo.astype(F32)], axis=0)
    out_ref[pl.ds(taps, 16), pl.ds(0, width)] = jnp.concatenate(
        [
            fused_hi.astype(F32),
            fused_lo.astype(F32),
            jnp.concatenate([last_rows, last_pad], axis=1),
            jnp.zeros((12, width), F32),
        ],
        axis=0,
    ).astype(BF16)
    out_ref[:, pl.ds(width, 2 * channels)] = lhs
    win_pad = jnp.zeros((block - channels, win.shape[1]), F32)
    out_ref[:, pl.ds(width + 128, win.shape[1])] = jnp.concatenate([win, win_pad], axis=0).astype(
        BF16
    )


def pack_kernel(
    plan, forcing_hbm, observed_hbm, sigma_hbm, class_hbm, cloud_hbm, count_hbm, x_ref, y_ref, w_ref,
    forcing_ref, observed_ref, sigma_ref, class_ref, cloud_ref, count_ref, sems,
):
    n_crops, local_crops, split, dup, layers = plan
    wait = fetch(
        [
            (class_hbm, class_ref),
            (forcing_hbm, forcing_ref),
            (observed_hbm, observed_ref),
            (sigma_hbm, sigma_ref.at[0]),
            (cloud_hbm, cloud_ref),
            (count_hbm, count_ref),
        ],
        sems,
    )
    wait()
    weeks, pixels = observed_ref.shape
    blocks = cloud_ref.shape[0]
    block_len = pixels // blocks
    member = lax.axis_index("member")
    local = member // split
    first_j, part = unit_place(plan, member)
    lane = lax.broadcasted_iota(jnp.int32, (1, pixels), 1)
    live = jnp.zeros((1, pixels), jnp.int32)
    for b in range(blocks):
        here = (lane >= b * block_len) & (lane < b * block_len + count_ref[b])
        live = jnp.where(here, 1, live)
    classes = class_ref[...]
    rank_of = lax.broadcasted_iota(jnp.int32, (CAP, pixels), 0)
    one_hots = []
    for n in range(n_crops):
        crop = unit_crop(plan, n, first_j) * local_crops + local
        one_hots.append(
            jnp.where((classes == crop * REGIONS + rank_of) & (live > 0), 1.0, 0.0).astype(F32)
        )
    hot = jnp.concatenate(one_hots, axis=0)
    if hot.shape[0] < 16:
        hot = jnp.concatenate([hot, jnp.zeros_like(hot)], axis=0)
    earlier = lax.broadcasted_iota(jnp.int32, (pixels, pixels), 0) < lax.broadcasted_iota(
        jnp.int32, (pixels, pixels), 1
    )
    rank = mm(hot.astype(BF16), jnp.where(earlier, 1.0, 0.0).astype(BF16))
    wanted = rank_of.astype(F32)
    if dup > 1:
        wanted = jnp.where(rank_of % dup == part, wanted, -1.0)
    selects = []
    for n in range(n_crops):
        rows = []
        for r in range(REGIONS):
            at = n * REGIONS + r
            match = (rank[at : at + 1] == wanted) & (hot[at : at + 1] > 0)
            rows.append(jnp.where(match, 1.0, 0.0))
        half = jnp.concatenate(rows, axis=0).astype(BF16)
        selects.append(jnp.concatenate([half, half], axis=0))
    select = jnp.concatenate(selects, axis=0)
    block_row = lax.broadcasted_iota(jnp.int32, (blocks, pixels), 0)
    block_lane = lax.broadcasted_iota(jnp.int32, (blocks, pixels), 1)
    in_block = (block_lane >= block_row * block_len) & (block_lane < (block_row + 1) * block_len)
    seen = lax.dot_general(
        cloud_ref[...].astype(F32),
        jnp.where(in_block, 1.0, 0.0),
        TN,
        preferred_element_type=F32,
    )
    weight = (seen / sigma_ref[...]).astype(BF16)
    observed = mm_nt(observed_ref[...], select)
    weight = mm_nt(weight, select)
    packed = mm_nt(forcing_ref[...], select)
    n_forcing = packed.shape[0] // weeks
    zero = jnp.zeros((n_forcing, LANES), F32)
    for n in range(n_crops):
        lanes = slice(n * LANES, (n + 1) * LANES)
        y_ref[n] = observed[:, lanes]
        w_ref[n] = weight[:, lanes]
        for t in range(weeks):
            now = packed[t * n_forcing : (t + 1) * n_forcing, lanes]
            for layer in range(layers):
                back = t - 2**layer
                then = packed[back * n_forcing : (back + 1) * n_forcing, lanes] if back >= 0 else zero
                x_ref[n, layer, :, pl.ds(t * LANES, LANES)] = jnp.concatenate(
                    [now, then], axis=0
                ).astype(BF16)


def unit_place(plan, member):
    n_crops, _, split, dup, _ = plan
    step = lax.rem(member, split)
    return (step // dup) * n_crops, lax.rem(step, dup)


def unit_crop(plan, n, first_j):
    return lax.rem(first_j + n + swap_base(plan), plan_shards(plan))


def swap_base(plan):
    return lax.axis_index("crop") if plan[0] == plan_shards(plan) else 0


def plan_shards(plan):
    return lax.axis_size("crop")


def net_kernel(dims, *refs):
    n_crops, my_members, layers, channels, blocks_in = dims
    refs = list(refs)
    x_ref, y_ref, w_ref = refs[:3]
    weight_refs = refs[3 : 3 + n_crops]
    theta_refs = refs[3 + n_crops : 3 + n_crops + blocks_in]
    out_ref, theta_out = refs[3 + n_crops + blocks_in : 5 + n_crops + blocks_in]
    theta_all, spread, base, inner0, inner1, bias_full, bias_now, pred = refs[
        5 + n_crops + blocks_in :
    ]
    members = theta_out.shape[0]
    pairs = members // 2
    weeks = y_ref.shape[1]
    span = 2 * LANES
    tiles = weeks // 2
    n_forcing = x_ref.shape[2] // 2
    taps, block = weight_rows(layers, channels)
    width = 2 * n_forcing + 2 * (layers - 1) * channels
    me = lax.axis_index("member")
    n_params = theta_out.shape[2]

    theta_all[...] = jnp.zeros(theta_all.shape, F32)
    for d, ref in enumerate(theta_refs):
        count = ref.shape[0]
        at = lax.rem(me + d, members // count) * count if blocks_in > 1 else 0
        for i in range(count):
            theta_all[at + i, :, pl.ds(n_forcing, n_params)] = ref[i]
            theta_out[at + i] = ref[i]

    for i in range(pairs):
        for half in range(2):
            for r in range(REGIONS):
                row = theta_all[i + half * pairs, pl.ds(r, 1), :]
                spread[pl.ds(i * LANES + half * SLOTS + r * CAP, CAP), :] = jnp.broadcast_to(
                    row, (CAP, row.shape[1])
                )
    spread_rows = spread[...].astype(BF16)

    def col(j):
        return pl.ds(j * span, span)

    lasts = []
    for n in range(n_crops):
        wts = weight_refs[n]
        stack = wts[:, pl.ds(width, 2 * channels)]
        now = stack[:taps, :channels]
        win = wts[pl.ds(0, channels), pl.ds(width + 128, n_forcing + n_params)]
        high, low = hi_lo(mm_nt(win, spread_rows))
        bias_full[n] = mm(
            jnp.concatenate([stack, stack], axis=1),
            jnp.concatenate([high, high, low, low], axis=0),
        )
        bias_now[n] = mm(
            jnp.concatenate([now, now], axis=1), jnp.concatenate([high, low], axis=0)
        )
        tail = wts[pl.ds(taps, 16), pl.ds(0, channels)].astype(F32)
        tail_row = tail[2:3] + tail[3:4]
        diag = lax.broadcasted_iota(jnp.int32, (channels, channels), 0) == lax.broadcasted_iota(
            jnp.int32, (channels, channels), 1
        )
        tail_col = jnp.sum(jnp.where(diag, tail_row, 0.0), axis=1, keepdims=True)
        lasts.append(jnp.broadcast_to(tail_col, (channels, span)))

    for n in range(n_crops):
        wts = weight_refs[n]
        last = lasts[n]
        first = wts[pl.ds(0, channels), pl.ds(0, 2 * n_forcing)]
        base[...] = mm(first, x_ref[n, 0])
        second = wts[pl.ds(channels, channels), pl.ds(0, 2 * n_forcing + 2 * channels)]
        third = wts[pl.ds(2 * channels, channels + 16), pl.ds(0, width)]
        zero_tile = jnp.zeros((channels, span), BF16)

        @pl.loop(0, pairs)
        def _(i):
            lanes = pl.ds(pl.multiple_of(i * LANES, LANES), LANES)

            def bias(layer, tile):
                rows = pl.ds(layer * channels, channels)
                parts = []
                for t in (2 * tile, 2 * tile + 1):
                    ref = bias_full if t >= 2**layer else bias_now
                    parts.append(ref[n, rows, lanes])
                return jnp.concatenate(parts, axis=1)

            def back(ref, tile):
                return ref[:, col(tile)] if tile >= 0 else zero_tile

            for j in range(tiles):
                inner0[:, col(j)] = jnp.maximum(base[:, col(j)] + bias(0, j), 0.0).astype(BF16)
            for j in range(tiles):
                rhs = jnp.concatenate(
                    [x_ref[n, 1, :, col(j)], inner0[:, col(j)], back(inner0, j - 1)], axis=0
                )
                inner1[:, col(j)] = jnp.maximum(mm(second, rhs) + bias(1, j), 0.0).astype(BF16)
            for j in range(tiles):
                rhs = jnp.concatenate(
                    [
                        x_ref[n, 2, :, col(j)],
                        inner0[:, col(j)],
                        back(inner0, j - 2),
                        inner1[:, col(j)],
                        back(inner1, j - 2),
                    ],
                    axis=0,
                )
                v = mm(third, rhs)
                h = jnp.maximum(v[:channels] + bias(2, j), 0.0) * last
                head_bias = bias_full[n, pl.ds(taps, 1), lanes]
                s = (
                    jnp.sum(h, axis=0, keepdims=True)
                    + v[channels : channels + 1]
                    + v[channels + 1 : channels + 2]
                    + jnp.concatenate([head_bias, head_bias], axis=1)
                )
                pred[2 * j, n, pl.ds(i, 1), :] = s[:, :LANES]
                pred[2 * j + 1, n, pl.ds(i, 1), :] = s[:, LANES:]

    lane = lax.broadcasted_iota(jnp.int32, (1, LANES), 1)
    low_half = lane < SLOTS
    region = (lane % SLOTS) // CAP
    masks = [jnp.where(region == r, 1.0, 0.0).astype(BF16) for r in range(REGIONS)]
    gram = jnp.zeros((REGIONS * members, members + 16), F32)
    held = []
    for t in range(weeks):
        scaled, innov = [], []
        for n in range(n_crops):
            p = pred[t, n]
            total = jnp.sum(p, axis=0, keepdims=True)
            mean = (total + pltpu.roll(total, SLOTS, 1)) / members
            w = w_ref[n, pl.ds(t, 1), :]
            y = y_ref[n, pl.ds(t, 1), :]
            scaled.append(w * (p - mean) / math.sqrt(ALPHA_INFLATION * (members - 1)))
            innov.append(w * (y - mean) / math.sqrt(ALPHA_INFLATION))
        if n_crops == 2:
            even = jnp.where(low_half, scaled[0], pltpu.roll(scaled[1], SLOTS, 1))
            odd = jnp.where(low_half, pltpu.roll(scaled[0], SLOTS, 1), scaled[1])
            row = jnp.where(low_half, innov[0], innov[1])
        else:
            even = jnp.where(low_half, scaled[0], 0.0)
            odd = jnp.where(low_half, pltpu.roll(scaled[0], SLOTS, 1), 0.0)
            row = jnp.where(low_half, innov[0], 0.0)
        rows = jnp.concatenate([even, odd], axis=0).astype(BF16)
        high, low = hi_lo(row)
        row_id = lax.broadcasted_iota(jnp.int32, (16, LANES), 0)
        extra = jnp.where(
            row_id == 0, high.astype(F32), jnp.where(row_id == 1, low.astype(F32), 0.0)
        ).astype(BF16)
        masked = jnp.concatenate([rows * mask for mask in masks], axis=0)
        held.append((masked, jnp.concatenate([rows, extra], axis=0)))
        if len(held) == 2:
            gram = gram + mm_nt(
                jnp.concatenate([h[0] for h in held], axis=1),
                jnp.concatenate([h[1] for h in held], axis=1),
            )
            held = []
    flat = jnp.transpose(gram)
    out_ref[...] = flat[: members + 8]


def solve_kernel(owned, gram_a, gram_b, theta_ref, out_ref, system, moved):
    members, _, n_params = theta_ref.shape
    my_members = out_ref.shape[0]
    first_region = lax.axis_index("crop") * owned
    first_member = lax.axis_index("member") * my_members
    gram = gram_a[...] + gram_b[...]
    for r in range(REGIONS):
        system[r] = gram[:, r * members : (r + 1) * members]
    row_id = lax.broadcasted_iota(jnp.int32, (members, 1), 0)
    eye = lax.broadcasted_iota(jnp.int32, (members, members), 0) == lax.broadcasted_iota(
        jnp.int32, (members, members), 1
    )
    scale_root = math.sqrt(members - 1)
    work = []
    for k in range(owned):
        block = system[first_region + k]
        g = block[:members]
        proj = block[members : members + 1] + block[members + 1 : members + 2]
        theta = jnp.concatenate(
            [theta_ref[m, pl.ds(first_region + k, 1), :] for m in range(members)], axis=0
        )
        spread = (theta - jnp.sum(theta, axis=0, keepdims=True) / members) / scale_root
        work.append([g + jnp.where(eye, 1.0, 0.0), spread, proj - scale_root * g, theta])
    for i in range(members):
        for item in work:
            a, z = item[0], item[1]
            column = a[:, i : i + 1]
            pivot = a[i : i + 1, i : i + 1]
            row_a = a[i : i + 1] / pivot
            row_z = z[i : i + 1] / pivot
            factor = jnp.where(row_id == i, column - 1.0, column)
            item[0] = a - factor * row_a
            item[1] = z - factor * row_z
    for k, (_, z, right, theta) in enumerate(work):
        moved[k] = theta + jnp.dot(
            right, z, precision=lax.Precision.HIGHEST, preferred_element_type=F32
        )
    for k in range(owned):
        for m in range(my_members):
            out_ref[m, pl.ds(k, 1), :] = moved[k, pl.ds(first_member + m, 1), :]


def local(
    forcing,
    observed,
    obs_sigma,
    pixel_class,
    pixel_count,
    cloud_free,
    params,
    input_weight,
    conv_weight,
    mix_weight,
    head_weight,
):
    n_crop = lax.axis_size("crop")
    n_member = lax.axis_size("member")
    weeks, n_forcing, pixels = forcing.shape
    local_crops, layers, channels, _ = conv_weight.shape
    my_members, _, n_params = params.shape
    members = my_members * n_member
    assert n_member % local_crops == 0
    split = n_member // local_crops
    dup = max(1, split // n_crop)
    n_crops = max(1, n_crop // split)
    assert n_crops in (1, 2) and n_crops * split == n_crop * dup
    plan = (n_crops, local_crops, split, dup, layers)
    params_kernel = pltpu.CompilerParams(vmem_limit_bytes=VMEM_LIMIT)
    taps, block = weight_rows(layers, channels)
    width = 2 * n_forcing + 2 * (layers - 1) * channels
    assert width % 16 == 0 and width + 2 * channels <= width + 128
    wide = -(-(width + 128 + n_forcing + n_params) // 128) * 128
    vmem_copy = lambda a: pltpu.VMEM(a.shape[1:], a.dtype)

    input_rows = jnp.swapaxes(input_weight, 1, 2)
    folded, theta_own = pl.pallas_call(
        functools.partial(fold_weights, split),
        out_shape=(
            jax.ShapeDtypeStruct((block, wide), BF16),
            jax.ShapeDtypeStruct(params.shape, F32),
        ),
        in_specs=hbm(5),
        out_specs=tuple(vmem(2)),
        scratch_shapes=[
            vmem_copy(input_rows),
            vmem_copy(conv_weight),
            vmem_copy(mix_weight),
            pltpu.VMEM(head_weight.shape, BF16),
            pltpu.VMEM((2 * channels, width), F32),
            pltpu.VMEM((block, 128), F32),
            pltpu.SemaphoreType.DMA((5,)),
        ],
        compiler_params=params_kernel,
    )(*stay(input_rows, conv_weight, mix_weight, head_weight, params))

    if n_crops == n_crop == 2:
        weights = [folded, lax.ppermute(folded, "crop", [(0, 1), (1, 0)])]
    else:
        gathered = lax.all_gather(folded, "crop", axis=0)
        first_j, _ = unit_place(plan, lax.axis_index("member"))
        weights = [
            lax.dynamic_index_in_dim(gathered, unit_crop(plan, n, first_j), 0, keepdims=False)
            for n in range(n_crops)
        ]
    if n_member <= 4:
        thetas = [theta_own] + [
            lax.ppermute(params, "member", [((i + d) % n_member, i) for i in range(n_member)])
            for d in range(1, n_member)
        ]
    else:
        thetas = [lax.all_gather(params, "member", axis=0, tiled=True)]

    x, y, w = pl.pallas_call(
        functools.partial(pack_kernel, plan),
        out_shape=(
            jax.ShapeDtypeStruct((n_crops, layers, 2 * n_forcing, weeks * LANES), BF16),
            jax.ShapeDtypeStruct((n_crops, weeks, LANES), F32),
            jax.ShapeDtypeStruct((n_crops, weeks, LANES), F32),
        ),
        in_specs=hbm(6),
        out_specs=tuple(vmem(3)),
        scratch_shapes=[
            pltpu.VMEM((weeks * n_forcing, pixels), BF16),
            pltpu.VMEM((weeks, pixels), BF16),
            pltpu.VMEM((1, pixels), F32),
            pltpu.VMEM((1, pixels), jnp.int32),
            pltpu.VMEM(cloud_free.shape, jnp.int32),
            pltpu.SMEM(pixel_count.shape, jnp.int32),
            pltpu.SemaphoreType.DMA((6,)),
        ],
        compiler_params=params_kernel,
    )(
        *stay(
            forcing.reshape(weeks * n_forcing, pixels),
            observed,
            obs_sigma,
            pixel_class.reshape(1, pixels),
            cloud_free,
            pixel_count,
        )
    )

    dims = (n_crops, my_members, layers, channels, len(thetas))
    pairs = members // 2
    gram, theta_all = pl.pallas_call(
        functools.partial(net_kernel, dims),
        out_shape=(
            jax.ShapeDtypeStruct((members + 8, REGIONS * members), F32),
            jax.ShapeDtypeStruct((members, REGIONS, n_params), F32),
        ),
        in_specs=vmem(3 + len(weights) + len(thetas)),
        out_specs=tuple(vmem(2)),
        scratch_shapes=[
            pltpu.VMEM((members, REGIONS, n_forcing + n_params), F32),
            pltpu.VMEM((pairs * LANES, n_forcing + n_params), F32),
            pltpu.VMEM((channels, weeks * LANES), F32),
            pltpu.VMEM((channels, weeks * LANES), BF16),
            pltpu.VMEM((channels, weeks * LANES), BF16),
            pltpu.VMEM((n_crops, block, pairs * LANES), F32),
            pltpu.VMEM((n_crops, taps, pairs * LANES), F32),
            pltpu.VMEM((weeks, n_crops, pairs, LANES), F32),
        ],
        compiler_params=params_kernel,
    )(x, y, w, *weights, *thetas)

    steps = []
    for axis in ("crop", "pixel", "member"):
        size = lax.axis_size(axis)
        d = 1
        while d < size:
            steps.append((axis, [(i, i ^ d) for i in range(size)]))
            d *= 2
    other = None
    for axis, pairs_ in steps:
        if other is not None:
            gram = gram + other
        other = lax.ppermute(gram, axis, pairs_)

    owned = REGIONS // n_crop
    return pl.pallas_call(
        functools.partial(solve_kernel, owned),
        out_shape=jax.ShapeDtypeStruct((my_members, owned, n_params), F32),
        in_specs=vmem(3),
        out_specs=vmem(1)[0],
        scratch_shapes=[
            pltpu.VMEM((REGIONS, members + 8, members), F32),
            pltpu.VMEM((owned, members, n_params), F32),
        ],
        compiler_params=params_kernel,
    )(gram, other, theta_all)


def solution(mesh):
    in_specs = (
        P(None, None, ("pixel", "crop")),
        P(None, ("pixel", "crop")),
        P(("pixel", "crop")),
        P(("pixel", "crop"), None),
        P(("pixel", "crop")),
        P(("pixel", "crop"), None),
        P("member", None, None),
        P("crop", None, None),
        P("crop", None, None, None),
        P("crop", None, None, None),
        P("crop", None),
    )
    out_specs = P("member", "crop", None)
    return jax.shard_map(local, mesh=mesh, in_specs=in_specs, out_specs=out_specs, check_vma=False)
```

time: 368 us -> 47.1 us (0.13)
  matrix products: 156 us -> 0 us
  blocking collectives: 82.7 us -> 0 us
  local copies, waits for them, and re-layouts: 39 us -> 0 us
  other arithmetic: 29.4 us -> 0.01 us
  waiting for transfers between devices: 37.7 us -> 15.6 us
  Pallas kernels: 0 us -> 19.2 us
  between operations: 13.7 us -> 0.04 us
  starting transfers between devices: 7.72 us -> 11.9 us
    dot_general x41 -> x0, matrix products: 155 us -> none  [the longest x12 75.5 us: run_network(): jnp.einsum('koc,tckq->tokq', mix_weight[:, layer], inner, preferred_eleme...]
    all_gather x4 -> x0, blocking collectives: 58.8 us -> none  [the longest x1 19.9 us: local(): shard_rows = lax.all_gather(scaled, 'member', axis=0, tiled=True)]
    psum x1 -> x0, waiting for transfers between devices: 33.1 us -> none  [local(): mean_pred = lax.psum(jnp.sum(predicted, axis=0), 'member') / members]
    psum x1 -> x0, blocking collectives: 23.8 us -> none  [local(): gram_sum, proj_sum = lax.psum((gram_rows, proj_rows), ('pixel', 'crop'))]
    slice x20 -> x0, local copies, waits for them, and re-layouts: 21.1 us -> none  [run_network(): hidden[:n_weeks - dilation]]
    pallas_call x0 -> x4, Pallas kernels: none -> 19.2 us  [the longest x1 14.1 us: local(): pl.pallas_call(functools.partial(net_kernel, dims), out_shape=(jax.ShapeD...]
    ppermute x0 -> x9, waiting for transfers between devices: none -> 15.6 us  [the longest x5 12.6 us: local(): other = lax.ppermute(gram, axis, pairs_)]
    another operation x9 -> x0, other arithmetic: 12.8 us -> none  [the longest x4 6.56 us: update(): factor = jnp.linalg.cholesky(system)]
  transfers between devices with their start and end apart: 3 -> 9, of which waited for: 2 -> 6; matrix products, arithmetic and copies ran while one was open for 3% -> 0% of each run, Pallas kernels for 0% -> 4%
where the time goes in v1:
time: 47.1 us; the launch traced here: 46.8 us
  Pallas kernels  19.2 us (41%)
  waiting for transfers between devices  15.6 us (33%)
  starting transfers between devices  11.9 us (25%)
    pallas_call x1, Pallas kernels, local(): pl.pallas_call(functools.partial(net_kernel, dims), out_shape=(jax.ShapeD...  14.1 us
    ppermute x5, waiting for transfers between devices, local(): other = lax.ppermute(gram, axis, pairs_)  12.6 us
    ppermute x3, starting transfers between devices, local(): lax.ppermute(params, 'member', [((i + d) % n_member, i) for i in range(n_...  4.62 us
    ppermute x5, starting transfers between devices, local(): other = lax.ppermute(gram, axis, pairs_)  4.29 us
    ppermute x3, waiting for transfers between devices, local(): lax.ppermute(params, 'member', [((i + d) % n_member, i) for i in range(n_...  3.04 us
    ppermute x1, starting transfers between devices, local(): weights = [folded, lax.ppermute(folded, 'crop', [(0, 1), (1, 0)])]  3 us
    pallas_call x1, Pallas kernels, local(): pl.pallas_call(functools.partial(solve_kernel, owned), out_shape=jax.Shap...  2.22 us
    pallas_call x1, Pallas kernels, local(): pl.pallas_call(functools.partial(pack_kernel, plan), out_shape=(jax.Shape...  1.68 us
  transfers between devices with their start and end apart: 9, of which 6 were waited for; matrix products, arithmetic and copies ran while one was open for 0% of the time, Pallas kernels for 4%

profile of v1, /device:TPU:0, one launch (start us, length us, event | category | flops | bytes accessed | tf_op | source)
XLA Modules:
  0.0 46.8 jit_solution(8639687314402259977)
XLA Ops:
  0.0 1.2 %shard_map.110 = (bf16[160,384]{1,0:T(8,128)(2,1)S(1)}, f32[4,8,24]{2,1,0:T(8,128)S(1)}) custom-call(bf16[4,32,48]{2,1,0:T(8,128)(2,1)} %bitcast.4, bf16[4,3,48,96]{3,2,1,0:T(8,128)(2,1)} %conv_hbm.1, bf16[4,3,48,48]{3,2,1,0:T(8,128)(2,1)} %mix_hbm.1, bf16[4,48]{1,0:T(4,128)(2,1)} %head_hbm.1, f32[4,8,24]{2,1,0:T(8,128)} %theta_hbm.1), custom_call_target="tpu_custom_call" | custom-call | tf_op jit(solution)/shard_map/pallas_call | solution.py:466
  1.2 3.0 %collective-permute-start = (bf16[160,384]{1,0:T(8,128)(2,1)S(1)}, bf16[160,384]{1,0:T(8,128)(2,1)S(1)}, u32[]{:S(2)}, u32[]{:S(2)}) collective-permute-start(bf16[160,384]{1,0:T(8,128)(2,1)S(1)} %get-tuple-element.15.refs_3_), channel_id=1, source_target_pairs={{0,4},{4,0},{1,5},{5,1},{2,6},{6,2},{3,7},{7,3},{8,12},{12,8},{9,1... | collective-permute-start | bytes 368648 | tf_op jit(solution)/shard_map/ppermute | solution.py:487
  4.2 3.6 %collective-permute-start.1 = (f32[4,8,24]{2,1,0:T(8,128)}, f32[4,8,24]{2,1,0:T(8,128)S(1)}, u32[]{:S(2)}, u32[]{:S(2)}) collective-permute-start(f32[4,8,24]{2,1,0:T(8,128)} %theta_hbm.1), channel_id=1, source_target_pairs={{1,0},{2,1},{3,2},{0,3},{5,4},{6,5},{7,6},{4,7},{9,8},{10,9},{11,1... | collective-permute-start | bytes 9224 | tf_op jit(solution)/shard_map/ppermute | solution.py:497
  7.8 0.0 collective-permute-start.3
  7.8 1.0 %collective-permute-start.2 = (f32[4,8,24]{2,1,0:T(8,128)}, f32[4,8,24]{2,1,0:T(8,128)S(1)}, u32[]{:S(2)}, u32[]{:S(2)}) collective-permute-start(f32[4,8,24]{2,1,0:T(8,128)} %theta_hbm.1), channel_id=1, source_target_pairs={{2,0},{3,1},{0,2},{1,3},{6,4},{7,5},{4,6},{5,7},{10,8},{11,9},{8,1... | collective-permute-start | bytes 9224 | tf_op jit(solution)/shard_map/ppermute | solution.py:497
  8.8 1.7 %shard_map.109 = (bf16[2,3,16,6656]{3,2,1,0:T(8,128)(2,1)S(1)}, f32[2,52,128]{2,1,0:T(8,128)S(1)}, f32[2,52,128]{2,1,0:T(8,128)S(1)}) custom-call(bf16[416,384]{1,0:T(8,128)(2,1)} %bitcast.3, bf16[52,384]{1,0:T(8,128)(2,1)} %observed_hbm.1, f32[384]{0:T(512)} %sigma_hbm.1, s32[1,384]{1,0:T(1,128)} %bitcast.5, s32[12,52]{1,0:T(8,128)} %cloud_hbm.1, s32[12]{0:T(128)} %count_hbm.1), custom_call_target="tpu_custom_call" | custom-call | tf_op jit(solution)/shard_map/pallas_call | solution.py:503
  10.5 0.0 collective-permute-done.1.refs_6_
  10.5 3.0 %collective-permute-done.3.refs_8_ = f32[4,8,24]{2,1,0:T(8,128)S(1)} collective-permute-done((f32[4,8,24]{2,1,0:T(8,128)}, f32[4,8,24]{2,1,0:T(8,128)S(1)}, u32[]{:S(2)}, u32[]{:S(2)}) %collective-permute-start.3) | collective-permute-done | bytes 3104 | tf_op jit(solution)/shard_map/ppermute | solution.py:497
  13.5 0.0 collective-permute-done.2.refs_7_
  13.5 0.0 collective-permute-done.refs_4_
  13.5 14.1 %shard_map.111 = (f32[24,128]{1,0:T(8,128)S(1)}, f32[16,8,24]{2,1,0:T(8,128)S(1)}) custom-call(bf16[2,3,16,6656]{3,2,1,0:T(8,128)(2,1)S(1)} %get-tuple-element.12.refs_0_, f32[2,52,128]{2,1,0:T(8,128)S(1)} %get-tuple-element.13.refs_1_, f32[2,52,128]{2,1,0:T(8,128)S(1)} %get-tuple-element.14.refs_2_, bf16[160,384]{1,0:T(8,128)(2,1)S(1)} %get-tuple-element.15.refs_3_, ...), custom_call_target="tpu_custom_call" | custom-call | tf_op jit(solution)/shard_map/pallas_call | solution.py:535
  27.7 0.6 %collective-permute-start.4 = (f32[24,128]{1,0:T(8,128)S(1)}, f32[24,128]{1,0:T(8,128)S(1)}, u32[]{:S(2)}, u32[]{:S(2)}) collective-permute-start(f32[24,128]{1,0:T(8,128)S(1)} %get-tuple-element.17), channel_id=1, source_target_pairs={{0,4},{4,0},{1,5},{5,1},{2,6},{6,2},{3,7},{7,3},{8,12},{12,8},{9,1... | collective-permute-start | bytes 36872 | tf_op jit(solution)/shard_map/ppermute | solution.py:567
  28.2 3.2 %collective-permute-done.4 = f32[24,128]{1,0:T(8,128)S(1)} collective-permute-done((f32[24,128]{1,0:T(8,128)S(1)}, f32[24,128]{1,0:T(8,128)S(1)}, u32[]{:S(2)}, u32[]{:S(2)}) %collective-permute-start.4) | collective-permute-done | bytes 12320 | tf_op jit(solution)/shard_map/ppermute | solution.py:567
  31.4 0.0 collective-permute-start.5
  31.4 1.2 %collective-permute-done.5 = f32[24,128]{1,0:T(8,128)S(1)} collective-permute-done((f32[24,128]{1,0:T(8,128)S(1)}, f32[24,128]{1,0:T(8,128)S(1)}, u32[]{:S(2)}, u32[]{:S(2)}) %collective-permute-start.5) | collective-permute-done | bytes 12320 | tf_op jit(solution)/shard_map/ppermute | solution.py:567
  32.6 1.5 %collective-permute-start.6 = (f32[24,128]{1,0:T(8,128)S(1)}, f32[24,128]{1,0:T(8,128)S(1)}, u32[]{:S(2)}, u32[]{:S(2)}) collective-permute-start(f32[24,128]{1,0:T(8,128)S(1)} %add.13), channel_id=1, source_target_pairs={{0,16},{8,24},{16,0},{24,8},{1,17},{9,25},{17,1},{25,9},{2,18},{10... | collective-permute-start | bytes 36872 | tf_op jit(solution)/shard_map/ppermute | solution.py:567
  34.1 2.2 %collective-permute-done.6 = f32[24,128]{1,0:T(8,128)S(1)} collective-permute-done((f32[24,128]{1,0:T(8,128)S(1)}, f32[24,128]{1,0:T(8,128)S(1)}, u32[]{:S(2)}, u32[]{:S(2)}) %collective-permute-start.6) | collective-permute-done | bytes 12320 | tf_op jit(solution)/shard_map/ppermute | solution.py:567
  36.3 0.7 %collective-permute-start.7 = (f32[24,128]{1,0:T(8,128)S(1)}, f32[24,128]{1,0:T(8,128)S(1)}, u32[]{:S(2)}, u32[]{:S(2)}) collective-permute-start(f32[24,128]{1,0:T(8,128)S(1)} %add.14), channel_id=1, source_target_pairs={{0,1},{1,0},{2,3},{3,2},{4,5},{5,4},{6,7},{7,6},{8,9},{9,8},{10,11... | collective-permute-start | bytes 36872 | tf_op jit(solution)/shard_map/ppermute | solution.py:567
  37.0 3.0 %collective-permute-done.7 = f32[24,128]{1,0:T(8,128)S(1)} collective-permute-done((f32[24,128]{1,0:T(8,128)S(1)}, f32[24,128]{1,0:T(8,128)S(1)}, u32[]{:S(2)}, u32[]{:S(2)}) %collective-permute-start.7) | collective-permute-done | bytes 12320 | tf_op jit(solution)/shard_map/ppermute | solution.py:567
  40.0 1.5 %collective-permute-start.8 = (f32[24,128]{1,0:T(8,128)S(1)}, f32[24,128]{1,0:T(8,128)S(1)}, u32[]{:S(2)}, u32[]{:S(2)}) collective-permute-start(f32[24,128]{1,0:T(8,128)S(1)} %add.15.gram_a), channel_id=1, source_target_pairs={{0,2},{1,3},{2,0},{3,1},{4,6},{5,7},{6,4},{7,5},{8,10},{9,11},{10,... | collective-permute-start | bytes 36872 | tf_op jit(solution)/shard_map/ppermute | solution.py:567
  41.5 3.1 %collective-permute-done.8.gram_b = f32[24,128]{1,0:T(8,128)S(1)} collective-permute-done((f32[24,128]{1,0:T(8,128)S(1)}, f32[24,128]{1,0:T(8,128)S(1)}, u32[]{:S(2)}, u32[]{:S(2)}) %collective-permute-start.8) | collective-permute-done | bytes 12320 | tf_op jit(solution)/shard_map/ppermute | solution.py:567
  44.6 2.2 %shard_map.112 = f32[4,4,24]{2,1,0:T(4,128)} custom-call(f32[24,128]{1,0:T(8,128)S(1)} %add.15.gram_a, f32[24,128]{1,0:T(8,128)S(1)} %collective-permute-done.8.gram_b, f32[16,8,24]{2,1,0:T(8,128)S(1)} %get-tuple-element.18.theta_ref), custom_call_target="tpu_custom_call" | custom-call | tf_op jit(solution)/shard_map/pallas_call | solution.py:570
  (4 shorter events, 0.0 us)
Async XLA Ops:
  1.2 12.4 %collective-permute-start = (bf16[160,384]{1,0:T(8,128)(2,1)S(1)}, bf16[160,384]{1,0:T(8,128)(2,1)S(1)}, u32[]{:S(2)}, u32[]{:S(2)}) collective-permute-start(bf16[160,384]{1,0:T(8,128)(2,1)S(1)} %get-tuple-element.15.refs_3_), channel_id=1, source_target_pairs={{0,4},{4,0},{1,5},{5,1},{2,6},{6,2},{3,7},{7,3},{8,12},{12,8},{9,1... | collective-permute-start | bytes 368648 | tf_op jit(solution)/shard_map/ppermute | solution.py:487
  4.2 6.3 %collective-permute-start.1 = (f32[4,8,24]{2,1,0:T(8,128)}, f32[4,8,24]{2,1,0:T(8,128)S(1)}, u32[]{:S(2)}, u32[]{:S(2)}) collective-permute-start(f32[4,8,24]{2,1,0:T(8,128)} %theta_hbm.1), channel_id=1, source_target_pairs={{1,0},{2,1},{3,2},{0,3},{5,4},{6,5},{7,6},{4,7},{9,8},{10,9},{11,1... | collective-permute-start | bytes 9224 | tf_op jit(solution)/shard_map/ppermute | solution.py:497
  7.8 5.7 %collective-permute-start.3 = (f32[4,8,24]{2,1,0:T(8,128)}, f32[4,8,24]{2,1,0:T(8,128)S(1)}, u32[]{:S(2)}, u32[]{:S(2)}) collective-permute-start(f32[4,8,24]{2,1,0:T(8,128)} %theta_hbm.1), channel_id=1, source_target_pairs={{3,0},{0,1},{1,2},{2,3},{7,4},{4,5},{5,6},{6,7},{11,8},{8,9},{9,10... | collective-permute-start | bytes 9224 | tf_op jit(solution)/shard_map/ppermute | solution.py:497
  7.8 5.7 %collective-permute-start.2 = (f32[4,8,24]{2,1,0:T(8,128)}, f32[4,8,24]{2,1,0:T(8,128)S(1)}, u32[]{:S(2)}, u32[]{:S(2)}) collective-permute-start(f32[4,8,24]{2,1,0:T(8,128)} %theta_hbm.1), channel_id=1, source_target_pairs={{2,0},{3,1},{0,2},{1,3},{6,4},{7,5},{4,6},{5,7},{10,8},{11,9},{8,1... | collective-permute-start | bytes 9224 | tf_op jit(solution)/shard_map/ppermute | solution.py:497
  27.7 3.7 %collective-permute-start.4 = (f32[24,128]{1,0:T(8,128)S(1)}, f32[24,128]{1,0:T(8,128)S(1)}, u32[]{:S(2)}, u32[]{:S(2)}) collective-permute-start(f32[24,128]{1,0:T(8,128)S(1)} %get-tuple-element.17), channel_id=1, source_target_pairs={{0,4},{4,0},{1,5},{5,1},{2,6},{6,2},{3,7},{7,3},{8,12},{12,8},{9,1... | collective-permute-start | bytes 36872 | tf_op jit(solution)/shard_map/ppermute | solution.py:567
  31.4 1.2 %collective-permute-start.5 = (f32[24,128]{1,0:T(8,128)S(1)}, f32[24,128]{1,0:T(8,128)S(1)}, u32[]{:S(2)}, u32[]{:S(2)}) collective-permute-start(f32[24,128]{1,0:T(8,128)S(1)} %add.12), channel_id=1, source_target_pairs={{0,8},{8,0},{16,24},{24,16},{1,9},{9,1},{17,25},{25,17},{2,10},{10... | collective-permute-start | bytes 36872 | tf_op jit(solution)/shard_map/ppermute | solution.py:567
  32.6 3.7 %collective-permute-start.6 = (f32[24,128]{1,0:T(8,128)S(1)}, f32[24,128]{1,0:T(8,128)S(1)}, u32[]{:S(2)}, u32[]{:S(2)}) collective-permute-start(f32[24,128]{1,0:T(8,128)S(1)} %add.13), channel_id=1, source_target_pairs={{0,16},{8,24},{16,0},{24,8},{1,17},{9,25},{17,1},{25,9},{2,18},{10... | collective-permute-start | bytes 36872 | tf_op jit(solution)/shard_map/ppermute | solution.py:567
  36.3 3.7 %collective-permute-start.7 = (f32[24,128]{1,0:T(8,128)S(1)}, f32[24,128]{1,0:T(8,128)S(1)}, u32[]{:S(2)}, u32[]{:S(2)}) collective-permute-start(f32[24,128]{1,0:T(8,128)S(1)} %add.14), channel_id=1, source_target_pairs={{0,1},{1,0},{2,3},{3,2},{4,5},{5,4},{6,7},{7,6},{8,9},{9,8},{10,11... | collective-permute-start | bytes 36872 | tf_op jit(solution)/shard_map/ppermute | solution.py:567
  40.0 4.6 %collective-permute-start.8 = (f32[24,128]{1,0:T(8,128)S(1)}, f32[24,128]{1,0:T(8,128)S(1)}, u32[]{:S(2)}, u32[]{:S(2)}) collective-permute-start(f32[24,128]{1,0:T(8,128)S(1)} %add.15.gram_a), channel_id=1, source_target_pairs={{0,2},{1,3},{2,0},{3,1},{4,6},{5,7},{6,4},{7,5},{8,10},{9,11},{10,... | collective-permute-start | bytes 36872 | tf_op jit(solution)/shard_map/ppermute | solution.py:567

commit v2 on v1

--- a/solution.py
+++ b/solution.py
@@ -13,6 +13,8 @@
 SLOTS = REGIONS * CAP
 LANES = 2 * SLOTS
 ALPHA_INFLATION = 4.0
+GROUP = 4
+BLOCK = 4
 VMEM_LIMIT = 48 * 2**20
 F32 = jnp.float32
 BF16 = jnp.bfloat16
@@ -40,6 +42,12 @@
 
 def hbm(n):
     return [pl.BlockSpec(memory_space=pltpu.HBM)] * n
+
+
+def cost(microseconds):
+    return pl.CostEstimate(
+        flops=int(microseconds * 1.1e9), bytes_accessed=int(microseconds * 3.5e6), transcendentals=0
+    )
 
 
 def stay(*arrays):
@@ -63,28 +71,13 @@
     return wait
 
 
-def fold_weights(
-    split, input_hbm, conv_hbm, mix_hbm, head_hbm, theta_hbm, out_ref, theta_ref,
-    input_ref, conv_ref, mix_ref, head_ref, quad, stack, sems,
-):
+def fold_weights(mine, input_ref, conv_ref, mix_ref, head_ref, out_ref, quad, stack):
     layers, channels = conv_ref.shape[0], conv_ref.shape[1]
     forcing = 8
-    mine = lax.axis_index("member") // split
-    wait = fetch(
-        [
-            (input_hbm.at[mine], input_ref),
-            (conv_hbm.at[mine], conv_ref),
-            (mix_hbm.at[mine], mix_ref),
-            (head_hbm, head_ref),
-            (theta_hbm, theta_ref),
-        ],
-        sems,
-    )
     taps, block = weight_rows(layers, channels)
     out_ref[...] = jnp.zeros(out_ref.shape, BF16)
     quad[...] = jnp.zeros(quad.shape, F32)
     stack[...] = jnp.zeros(stack.shape, F32)
-    wait()
     win = jnp.transpose(input_ref[...].astype(F32))
     for half in range(2):
         rows = pl.ds(half * channels, channels)
@@ -126,23 +119,23 @@
     )
 
 
-def pack_kernel(
-    plan, forcing_hbm, observed_hbm, sigma_hbm, class_hbm, cloud_hbm, count_hbm, x_ref, y_ref, w_ref,
-    forcing_ref, observed_ref, sigma_ref, class_ref, cloud_ref, count_ref, sems,
+def prepare(plan, *refs):
+    sources, refs = refs[:11], refs[11:]
+    folded, theta, x, y, w = refs[:5]
+    buffers, (quad, stack, sems) = refs[5:15], refs[15:]
+    mine = lax.axis_index("member") // plan[2]
+    sliced = [s.at[mine] if i < 3 else s for i, s in enumerate(sources)]
+    copies = list(zip(sliced, buffers[:4] + (theta,) + buffers[4:]))
+    copies[7] = (copies[7][0], copies[7][1].at[0])
+    fetch(copies, sems)()
+    fold_weights(mine, *buffers[:4], folded, quad, stack)
+    pack_slots(plan, *buffers[4:], x, y, w)
+
+
+def pack_slots(
+    plan, forcing_ref, observed_ref, sigma_ref, class_ref, cloud_ref, count_ref, x_ref, y_ref, w_ref
 ):
     n_crops, local_crops, split, dup, layers = plan
-    wait = fetch(
-        [
-            (class_hbm, class_ref),
-            (forcing_hbm, forcing_ref),
-            (observed_hbm, observed_ref),
-            (sigma_hbm, sigma_ref.at[0]),
-            (cloud_hbm, cloud_ref),
-            (count_hbm, count_ref),
-        ],
-        sems,
-    )
-    wait()
     weeks, pixels = observed_ref.shape
     blocks = cloud_ref.shape[0]
     block_len = pixels // blocks
@@ -229,31 +222,21 @@
     return lax.axis_size("crop")
 
 
-def net_kernel(dims, *refs):
-    n_crops, my_members, layers, channels, blocks_in = dims
-    refs = list(refs)
-    x_ref, y_ref, w_ref = refs[:3]
-    weight_refs = refs[3 : 3 + n_crops]
-    theta_refs = refs[3 + n_crops : 3 + n_crops + blocks_in]
-    out_ref, theta_out = refs[3 + n_crops + blocks_in : 5 + n_crops + blocks_in]
-    theta_all, spread, base, inner0, inner1, bias_full, bias_now, pred = refs[
-        5 + n_crops + blocks_in :
-    ]
-    members = theta_out.shape[0]
+def net_first(dims, *refs):
+    blocks_in, n_forcing = dims
+    x_ref, wts = refs[:2]
+    theta_refs, refs = refs[2 : 2 + blocks_in], refs[2 + blocks_in :]
+    pred, theta_out, spread = refs[:3]
+    theta_all = refs[3]
+    scratch = refs[4:]
+    members, _, n_params = theta_out.shape
     pairs = members // 2
-    weeks = y_ref.shape[1]
-    span = 2 * LANES
-    tiles = weeks // 2
-    n_forcing = x_ref.shape[2] // 2
-    taps, block = weight_rows(layers, channels)
-    width = 2 * n_forcing + 2 * (layers - 1) * channels
     me = lax.axis_index("member")
-    n_params = theta_out.shape[2]
 
     theta_all[...] = jnp.zeros(theta_all.shape, F32)
     for d, ref in enumerate(theta_refs):
         count = ref.shape[0]
-        at = lax.rem(me + d, members // count) * count if blocks_in > 1 else 0
+        at = (me ^ d) * count if blocks_in > 1 else 0
         for i in range(count):
             theta_all[at + i, :, pl.ds(n_forcing, n_params)] = ref[i]
             theta_out[at + i] = ref[i]
@@ -265,86 +248,133 @@
                 spread[pl.ds(i * LANES + half * SLOTS + r * CAP, CAP), :] = jnp.broadcast_to(
                     row, (CAP, row.shape[1])
                 )
-    spread_rows = spread[...].astype(BF16)
+    run_crop(x_ref, 0, wts, spread, pred, *scratch)
+
+
+def run_crop(x_ref, n, wts, spread, pred, base, inner0, inner1, bias_full, bias_now):
+    layers, n_forcing = x_ref.shape[1], x_ref.shape[2] // 2
+    channels = base.shape[0]
+    taps, block = weight_rows(layers, channels)
+    width = 2 * n_forcing + 2 * (layers - 1) * channels
+    pairs = pred.shape[1]
+    tiles = pred.shape[0] // 2
+    span = 2 * LANES
 
     def col(j):
         return pl.ds(j * span, span)
 
-    lasts = []
-    for n in range(n_crops):
-        wts = weight_refs[n]
-        stack = wts[:, pl.ds(width, 2 * channels)]
-        now = stack[:taps, :channels]
-        win = wts[pl.ds(0, channels), pl.ds(width + 128, n_forcing + n_params)]
-        high, low = hi_lo(mm_nt(win, spread_rows))
-        bias_full[n] = mm(
-            jnp.concatenate([stack, stack], axis=1),
-            jnp.concatenate([high, high, low, low], axis=0),
-        )
-        bias_now[n] = mm(
-            jnp.concatenate([now, now], axis=1), jnp.concatenate([high, low], axis=0)
-        )
-        tail = wts[pl.ds(taps, 16), pl.ds(0, channels)].astype(F32)
-        tail_row = tail[2:3] + tail[3:4]
-        diag = lax.broadcasted_iota(jnp.int32, (channels, channels), 0) == lax.broadcasted_iota(
-            jnp.int32, (channels, channels), 1
-        )
-        tail_col = jnp.sum(jnp.where(diag, tail_row, 0.0), axis=1, keepdims=True)
-        lasts.append(jnp.broadcast_to(tail_col, (channels, span)))
-
-    for n in range(n_crops):
-        wts = weight_refs[n]
-        last = lasts[n]
-        first = wts[pl.ds(0, channels), pl.ds(0, 2 * n_forcing)]
-        base[...] = mm(first, x_ref[n, 0])
-        second = wts[pl.ds(channels, channels), pl.ds(0, 2 * n_forcing + 2 * channels)]
-        third = wts[pl.ds(2 * channels, channels + 16), pl.ds(0, width)]
-        zero_tile = jnp.zeros((channels, span), BF16)
-
-        @pl.loop(0, pairs)
-        def _(i):
-            lanes = pl.ds(pl.multiple_of(i * LANES, LANES), LANES)
-
-            def bias(layer, tile):
-                rows = pl.ds(layer * channels, channels)
+    stack = wts[:, pl.ds(width, 2 * channels)]
+    now = stack[:taps, :channels]
+    win = wts[pl.ds(0, channels), pl.ds(width + 128, spread.shape[1])]
+    high, low = hi_lo(mm_nt(win, spread[...].astype(BF16)))
+    bias_full[...] = mm(
+        jnp.concatenate([stack, stack], axis=1),
+        jnp.concatenate([high, high, low, low], axis=0),
+    )
+    bias_now[...] = mm(
+        jnp.concatenate([now, now], axis=1), jnp.concatenate([high, low], axis=0)
+    )
+    tail = wts[pl.ds(taps, 16), pl.ds(0, channels)].astype(F32)
+    tail_row = tail[2:3] + tail[3:4]
+    diag = lax.broadcasted_iota(jnp.int32, (channels, channels), 0) == lax.broadcasted_iota(
+        jnp.int32, (channels, channels), 1
+    )
+    tail_col = jnp.sum(jnp.where(diag, tail_row, 0.0), axis=1, keepdims=True)
+    last = jnp.broadcast_to(tail_col, (channels, LANES))
+    first = wts[pl.ds(0, channels), pl.ds(0, 2 * n_forcing)]
+    base[...] = mm(first, x_ref[n, 0])
+    second = wts[pl.ds(channels, channels), pl.ds(0, 2 * n_forcing + 2 * channels)]
+    third = wts[pl.ds(2 * channels, channels + 16), pl.ds(0, width)]
+    zero_tile = jnp.zeros((channels, span), BF16)
+
+    group = inner0.shape[0]
+
+    @pl.loop(0, pairs // group)
+    def _(step):
+        items = [step * group + u for u in range(group)]
+        lanes = [pl.ds(pl.multiple_of(i * LANES, LANES), LANES) for i in items]
+
+        def bias_of(u, layer):
+            rows = pl.ds(layer * channels, channels)
+            seen = {}
+
+            def get(tile):
                 parts = []
                 for t in (2 * tile, 2 * tile + 1):
-                    ref = bias_full if t >= 2**layer else bias_now
-                    parts.append(ref[n, rows, lanes])
+                    late = t >= 2**layer
+                    if late not in seen:
+                        seen[late] = (bias_full if late else bias_now)[rows, lanes[u]]
+                    parts.append(seen[late])
                 return jnp.concatenate(parts, axis=1)
 
-            def back(ref, tile):
-                return ref[:, col(tile)] if tile >= 0 else zero_tile
-
-            for j in range(tiles):
-                inner0[:, col(j)] = jnp.maximum(base[:, col(j)] + bias(0, j), 0.0).astype(BF16)
-            for j in range(tiles):
+            return get
+
+        def back(ref, u, tile):
+            return ref[u, :, col(tile)] if tile >= 0 else zero_tile
+
+        def layer0(block_tiles):
+            for j in block_tiles:
+                shared = base[:, col(j)]
+                for u in range(group):
+                    inner0[u, :, col(j)] = jnp.maximum(shared + bias_of(u, 0)(j), 0.0).astype(BF16)
+
+        def layer1(u, block_tiles):
+            bias = bias_of(u, 1)
+            for j in block_tiles:
                 rhs = jnp.concatenate(
-                    [x_ref[n, 1, :, col(j)], inner0[:, col(j)], back(inner0, j - 1)], axis=0
+                    [x_ref[n, 1, :, col(j)], inner0[u, :, col(j)], back(inner0, u, j - 1)], axis=0
                 )
-                inner1[:, col(j)] = jnp.maximum(mm(second, rhs) + bias(1, j), 0.0).astype(BF16)
-            for j in range(tiles):
+                inner1[u, :, col(j)] = jnp.maximum(mm(second, rhs) + bias(j), 0.0).astype(BF16)
+
+        def layer2(u, block_tiles):
+            bias = bias_of(u, 2)
+            head_bias = bias_full[pl.ds(taps, 1), lanes[u]]
+            for j in block_tiles:
                 rhs = jnp.concatenate(
                     [
                         x_ref[n, 2, :, col(j)],
-                        inner0[:, col(j)],
-                        back(inner0, j - 2),
-                        inner1[:, col(j)],
-                        back(inner1, j - 2),
+                        inner0[u, :, col(j)],
+                        back(inner0, u, j - 2),
+                        inner1[u, :, col(j)],
+                        back(inner1, u, j - 2),
                     ],
                     axis=0,
                 )
                 v = mm(third, rhs)
-                h = jnp.maximum(v[:channels] + bias(2, j), 0.0) * last
-                head_bias = bias_full[n, pl.ds(taps, 1), lanes]
+                h = jnp.maximum(v[:channels] + bias(j), 0.0) * jnp.concatenate([last, last], axis=1)
                 s = (
                     jnp.sum(h, axis=0, keepdims=True)
                     + v[channels : channels + 1]
                     + v[channels + 1 : channels + 2]
                     + jnp.concatenate([head_bias, head_bias], axis=1)
                 )
-                pred[2 * j, n, pl.ds(i, 1), :] = s[:, :LANES]
-                pred[2 * j + 1, n, pl.ds(i, 1), :] = s[:, LANES:]
+                pred[2 * j, pl.ds(items[u], 1), :] = s[:, :LANES]
+                pred[2 * j + 1, pl.ds(items[u], 1), :] = s[:, LANES:]
+
+        blocks = [range(j, min(j + BLOCK, tiles)) for j in range(0, tiles, BLOCK)]
+        for step_at in range(len(blocks) + 2):
+            if step_at < len(blocks):
+                layer0(blocks[step_at])
+            for u in range(group):
+                if 0 <= step_at - 1 < len(blocks):
+                    layer1(u, blocks[step_at - 1])
+                if 0 <= step_at - 2 < len(blocks):
+                    layer2(u, blocks[step_at - 2])
+
+
+def net_last(n_crops, *refs):
+    x_ref, y_ref, w_ref, pred_first = refs[:4]
+    refs = refs[4:]
+    preds = [pred_first]
+    if n_crops == 2:
+        wts, spread = refs[:2]
+        out_ref, pred = refs[2:4]
+        run_crop(x_ref, 1, wts, spread, pred, *refs[4:])
+        preds.append(pred)
+    else:
+        out_ref = refs[0]
+    weeks = y_ref.shape[1]
+    members = 2 * pred_first.shape[1]
 
     lane = lax.broadcasted_iota(jnp.int32, (1, LANES), 1)
     low_half = lane < SLOTS
@@ -355,7 +385,7 @@
     for t in range(weeks):
         scaled, innov = [], []
         for n in range(n_crops):
-            p = pred[t, n]
+            p = preds[n][t]
             total = jnp.sum(p, axis=0, keepdims=True)
             mean = (total + pltpu.roll(total, SLOTS, 1)) / members
             w = w_ref[n, pl.ds(t, 1), :]
@@ -463,25 +493,49 @@
     vmem_copy = lambda a: pltpu.VMEM(a.shape[1:], a.dtype)
 
     input_rows = jnp.swapaxes(input_weight, 1, 2)
-    folded, theta_own = pl.pallas_call(
-        functools.partial(fold_weights, split),
+    folded, theta_own, x, y, w = pl.pallas_call(
+        functools.partial(prepare, plan),
         out_shape=(
             jax.ShapeDtypeStruct((block, wide), BF16),
             jax.ShapeDtypeStruct(params.shape, F32),
+            jax.ShapeDtypeStruct((n_crops, layers, 2 * n_forcing, weeks * LANES), BF16),
+            jax.ShapeDtypeStruct((n_crops, weeks, LANES), F32),
+            jax.ShapeDtypeStruct((n_crops, weeks, LANES), F32),
         ),
-        in_specs=hbm(5),
-        out_specs=tuple(vmem(2)),
+        in_specs=hbm(11),
+        out_specs=tuple(vmem(5)),
         scratch_shapes=[
             vmem_copy(input_rows),
             vmem_copy(conv_weight),
             vmem_copy(mix_weight),
             pltpu.VMEM(head_weight.shape, BF16),
+            pltpu.VMEM((weeks * n_forcing, pixels), BF16),
+            pltpu.VMEM((weeks, pixels), BF16),
+            pltpu.VMEM((1, pixels), F32),
+            pltpu.VMEM((1, pixels), jnp.int32),
+            pltpu.VMEM(cloud_free.shape, jnp.int32),
+            pltpu.SMEM(pixel_count.shape, jnp.int32),
             pltpu.VMEM((2 * channels, width), F32),
             pltpu.VMEM((block, 128), F32),
-            pltpu.SemaphoreType.DMA((5,)),
+            pltpu.SemaphoreType.DMA((11,)),
         ],
         compiler_params=params_kernel,
-    )(*stay(input_rows, conv_weight, mix_weight, head_weight, params))
+        cost_estimate=cost(2),
+    )(
+        *stay(
+            input_rows,
+            conv_weight,
+            mix_weight,
+            head_weight,
+            params,
+            forcing.reshape(weeks * n_forcing, pixels),
+            observed,
+            obs_sigma,
+            pixel_class.reshape(1, pixels),
+            cloud_free,
+            pixel_count,
+        )
+    )
 
     if n_crops == n_crop == 2:
         weights = [folded, lax.ppermute(folded, "crop", [(0, 1), (1, 0)])]
@@ -492,66 +546,49 @@
             lax.dynamic_index_in_dim(gathered, unit_crop(plan, n, first_j), 0, keepdims=False)
             for n in range(n_crops)
         ]
-    if n_member <= 4:
+    if n_member in (2, 4):
         thetas = [theta_own] + [
-            lax.ppermute(params, "member", [((i + d) % n_member, i) for i in range(n_member)])
+            lax.ppermute(params, "member", [(i, i ^ d) for i in range(n_member)])
             for d in range(1, n_member)
         ]
     else:
         thetas = [lax.all_gather(params, "member", axis=0, tiled=True)]
 
-    x, y, w = pl.pallas_call(
-        functools.partial(pack_kernel, plan),
+    pairs = members // 2
+    group = math.gcd(pairs, GROUP)
+    scratch = [
+        pltpu.VMEM((channels, weeks * LANES), F32),
+        pltpu.VMEM((group, channels, weeks * LANES), BF16),
+        pltpu.VMEM((group, channels, weeks * LANES), BF16),
+        pltpu.VMEM((block, pairs * LANES), F32),
+        pltpu.VMEM((taps, pairs * LANES), F32),
+    ]
+    pred, theta_all, spread = pl.pallas_call(
+        functools.partial(net_first, (len(thetas), n_forcing)),
         out_shape=(
-            jax.ShapeDtypeStruct((n_crops, layers, 2 * n_forcing, weeks * LANES), BF16),
-            jax.ShapeDtypeStruct((n_crops, weeks, LANES), F32),
-            jax.ShapeDtypeStruct((n_crops, weeks, LANES), F32),
+            jax.ShapeDtypeStruct((weeks, pairs, LANES), F32),
+            jax.ShapeDtypeStruct((members, REGIONS, n_params), F32),
+            jax.ShapeDtypeStruct((pairs * LANES, n_forcing + n_params), F32),
         ),
-        in_specs=hbm(6),
+        in_specs=vmem(2 + len(thetas)),
         out_specs=tuple(vmem(3)),
-        scratch_shapes=[
-            pltpu.VMEM((weeks * n_forcing, pixels), BF16),
-            pltpu.VMEM((weeks, pixels), BF16),
-            pltpu.VMEM((1, pixels), F32),
-            pltpu.VMEM((1, pixels), jnp.int32),
-            pltpu.VMEM(cloud_free.shape, jnp.int32),
-            pltpu.SMEM(pixel_count.shape, jnp.int32),
-            pltpu.SemaphoreType.DMA((6,)),
-        ],
+        scratch_shapes=[pltpu.VMEM((members, REGIONS, n_forcing + n_params), F32)] + scratch,
         compiler_params=params_kernel,
-    )(
-        *stay(
-            forcing.reshape(weeks * n_forcing, pixels),
-            observed,
-            obs_sigma,
-            pixel_class.reshape(1, pixels),
-            cloud_free,
-            pixel_count,
-        )
-    )
-
-    dims = (n_crops, my_members, layers, channels, len(thetas))
-    pairs = members // 2
-    gram, theta_all = pl.pallas_call(
-        functools.partial(net_kernel, dims),
-        out_shape=(
-            jax.ShapeDtypeStruct((members + 8, REGIONS * members), F32),
-            jax.ShapeDtypeStruct((members, REGIONS, n_params), F32),
-        ),
-        in_specs=vmem(3 + len(weights) + len(thetas)),
-        out_specs=tuple(vmem(2)),
-        scratch_shapes=[
-            pltpu.VMEM((members, REGIONS, n_forcing + n_params), F32),
-            pltpu.VMEM((pairs * LANES, n_forcing + n_params), F32),
-            pltpu.VMEM((channels, weeks * LANES), F32),
-            pltpu.VMEM((channels, weeks * LANES), BF16),
-            pltpu.VMEM((channels, weeks * LANES), BF16),
-            pltpu.VMEM((n_crops, block, pairs * LANES), F32),
-            pltpu.VMEM((n_crops, taps, pairs * LANES), F32),
-            pltpu.VMEM((weeks, n_crops, pairs, LANES), F32),
-        ],
+        cost_estimate=cost(7),
+    )(x, weights[0], *thetas)
+    rest = [x, y, w, pred]
+    scratch = [pltpu.VMEM((weeks, pairs, LANES), F32)] + scratch
+    if n_crops == 2:
+        rest += [weights[1], spread]
+    gram = pl.pallas_call(
+        functools.partial(net_last, n_crops),
+        out_shape=jax.ShapeDtypeStruct((members + 8, REGIONS * members), F32),
+        in_specs=vmem(len(rest)),
+        out_specs=vmem(1)[0],
+        scratch_shapes=scratch if n_crops == 2 else [],
         compiler_params=params_kernel,
-    )(x, y, w, *weights, *thetas)
+        cost_estimate=cost(8),
+    )(*rest)
 
     steps = []
     for axis in ("crop", "pixel", "member"):
@@ -577,6 +614,7 @@
             pltpu.VMEM((owned, members, n_params), F32),
         ],
         compiler_params=params_kernel,
+        cost_estimate=cost(2),
     )(gram, other, theta_all)
 
 

time: 47.1 us -> 43 us (0.913)
  Pallas kernels: 19.2 us -> 16.5 us
  starting transfers between devices: 11.9 us -> 10.6 us
    pallas_call x3, Pallas kernels: 17 us -> 14.3 us  [the longest x1 6.58 us: local(): pl.pallas_call(functools.partial(net_last, n_crops), out_shape=jax.ShapeD...]
    ppermute x1, starting transfers between devices: 3 us -> 1.77 us  [local(): weights = [folded, lax.ppermute(folded, 'crop', [(0, 1), (1, 0)])]]
    ppermute x3, waiting for transfers between devices: 3.04 us -> 1.97 us  [local(): lax.ppermute(params, 'member', [(i, i ^ d) for i in range(n_member)])]
    ppermute x5, waiting for transfers between devices: 12.6 us -> 13.6 us  [local(): other = lax.ppermute(gram, axis, pairs_)]
    ppermute x5, starting transfers between devices: 4.29 us -> 3.27 us  [local(): other = lax.ppermute(gram, axis, pairs_)]
    ppermute x3, starting transfers between devices: 4.62 us -> 5.62 us  [local(): lax.ppermute(params, 'member', [(i, i ^ d) for i in range(n_member)])]
  transfers between devices with their start and end apart: 9 -> 9, of which waited for: 6 -> 6; matrix products, arithmetic and copies ran while one was open for 0% -> 0% of each run, Pallas kernels for 4% -> 18%
where the time goes in v2:
time: 43 us; the launch traced here: 42.8 us
  Pallas kernels  16.5 us (38%)
  waiting for transfers between devices  15.6 us (36%)
  starting transfers between devices  10.6 us (25%)
    ppermute x5, waiting for transfers between devices, local(): other = lax.ppermute(gram, axis, pairs_)  13.6 us
    pallas_call x1, Pallas kernels, local(): pl.pallas_call(functools.partial(net_last, n_crops), out_shape=jax.ShapeD...  6.58 us
    pallas_call x1, Pallas kernels, local(): pl.pallas_call(functools.partial(net_first, (len(thetas), n_forcing)), ou...  5.72 us
    ppermute x3, starting transfers between devices, local(): lax.ppermute(params, 'member', [(i, i ^ d) for i in range(n_member)])  5.62 us
    ppermute x5, starting transfers between devices, local(): other = lax.ppermute(gram, axis, pairs_)  3.27 us
    pallas_call x1, Pallas kernels, local(): pl.pallas_call(functools.partial(solve_kernel, owned), out_shape=jax.Shap...  2.22 us
    pallas_call x1, Pallas kernels, local(): pl.pallas_call(functools.partial(prepare, plan), out_shape=(jax.ShapeDtyp...  2 us
    ppermute x3, waiting for transfers between devices, local(): lax.ppermute(params, 'member', [(i, i ^ d) for i in range(n_member)])  1.97 us
  transfers between devices with their start and end apart: 9, of which 6 were waited for; matrix products, arithmetic and copies ran while one was open for 0% of the time, Pallas kernels for 18%

profile of v2, /device:TPU:0, one launch (start us, length us, event | category | flops | bytes accessed | tf_op | source)
XLA Modules:
  0.0 42.8 jit_solution(907937783901932393)
XLA Ops:
  0.0 3.0 %collective-permute-start = (f32[4,8,24]{2,1,0:T(8,128)}, f32[4,8,24]{2,1,0:T(8,128)S(1)}, u32[]{:S(2)}, u32[]{:S(2)}) collective-permute-start(f32[4,8,24]{2,1,0:T(8,128)} %refs_4_.1), channel_id=1, source_target_pairs={{0,1},{1,0},{2,3},{3,2},{4,5},{5,4},{6,7},{7,6},{8,9},{9,8},{10,11... | collective-permute-start | bytes 9224 | tf_op jit(solution)/shard_map/ppermute | solution.py:551
  3.0 2.6 %collective-permute-start.1 = (f32[4,8,24]{2,1,0:T(8,128)}, f32[4,8,24]{2,1,0:T(8,128)S(1)}, u32[]{:S(2)}, u32[]{:S(2)}) collective-permute-start(f32[4,8,24]{2,1,0:T(8,128)} %refs_4_.1), channel_id=1, source_target_pairs={{0,2},{1,3},{2,0},{3,1},{4,6},{5,7},{6,4},{7,5},{8,10},{9,11},{10,... | collective-permute-start | bytes 9224 | tf_op jit(solution)/shard_map/ppermute | solution.py:551
  5.6 0.0 collective-permute-start.2
  5.6 2.0 %shard_map.109 = (bf16[160,384]{1,0:T(8,128)(2,1)S(1)}, f32[4,8,24]{2,1,0:T(8,128)S(1)}, bf16[2,3,16,6656]{3,2,1,0:T(8,128)(2,1)S(1)}, f32[2,52,128]{2,1,0:T(8,128)S(1)}, f32[2,52,128]{2,1,0:T(8,128)S(1)}) custom-call(bf16[4,32,48]{2,1,0:T(8,128)(2,1)} %bitcast.4, bf16[4,3,48,96]{3,2,1,0:T(8,128)(2,1)} %refs_1_.1, bf16[4,3,48,48]{3,2,1,0:T(8,128)(2,1)} %refs_2_.1, ...), custom_call_target="tpu_custom_call" | custom-call | flops 2200000000 | bytes 7000000 | tf_op jit(solution)/shard_map/pallas_call | solution.py:496
  7.6 1.8 %collective-permute-start.3 = (bf16[160,384]{1,0:T(8,128)(2,1)S(1)}, bf16[160,384]{1,0:T(8,128)(2,1)S(1)}, u32[]{:S(2)}, u32[]{:S(2)}) collective-permute-start(bf16[160,384]{1,0:T(8,128)(2,1)S(1)} %get-tuple-element.16.refs_1_), channel_id=1, source_target_pairs={{0,4},{4,0},{1,5},{5,1},{2,6},{6,2},{3,7},{7,3},{8,12},{12,8},{9,1... | collective-permute-start | bytes 368648 | tf_op jit(solution)/shard_map/ppermute | solution.py:541
  9.4 0.0 collective-permute-done.refs_3_
  9.4 0.0 collective-permute-done.1.refs_4_
  9.4 2.0 %collective-permute-done.2.refs_5_ = f32[4,8,24]{2,1,0:T(8,128)S(1)} collective-permute-done((f32[4,8,24]{2,1,0:T(8,128)}, f32[4,8,24]{2,1,0:T(8,128)S(1)}, u32[]{:S(2)}, u32[]{:S(2)}) %collective-permute-start.2) | collective-permute-done | bytes 3104 | tf_op jit(solution)/shard_map/ppermute | solution.py:551
  11.4 5.7 %shard_map.110 = (f32[52,8,128]{2,1,0:T(8,128)S(1)}, f32[16,8,24]{2,1,0:T(8,128)S(1)}, f32[1024,32]{1,0:T(8,128)S(1)}) custom-call(bf16[2,3,16,6656]{3,2,1,0:T(8,128)(2,1)S(1)} %get-tuple-element.13.refs_0_, bf16[160,384]{1,0:T(8,128)(2,1)S(1)} %get-tuple-element.16.refs_1_, f32[4,8,24]{2,1,0:T(8,128)S(1)} %get-tuple-element.17.refs_2_, ...), custom_call_target="tpu_custom_call" | custom-call | flops 7699999744 | bytes 24500000 | tf_op jit(solution)/shard_map/pallas_call | solution.py:566
  17.1 0.0 collective-permute-done.3.refs_4_
  17.1 6.6 %shard_map.111 = f32[24,128]{1,0:T(8,128)S(1)} custom-call(bf16[2,3,16,6656]{3,2,1,0:T(8,128)(2,1)S(1)} %get-tuple-element.13.refs_0_, f32[2,52,128]{2,1,0:T(8,128)S(1)} %get-tuple-element.14.refs_1_, f32[2,52,128]{2,1,0:T(8,128)S(1)} %get-tuple-element.15.refs_2_, f32[52,8,128]{2,1,0:T(8,128)S(1)} %get-tuple-element.18.refs_3_, ...), custom_call_target="tpu_custom_call" | custom-call | flops 8800000000 | bytes 28000000 | tf_op jit(solution)/shard_map/pallas_call | solution.py:583
  23.7 1.5 %collective-permute-start.4 = (f32[24,128]{1,0:T(8,128)S(1)}, f32[24,128]{1,0:T(8,128)S(1)}, u32[]{:S(2)}, u32[]{:S(2)}) collective-permute-start(f32[24,128]{1,0:T(8,128)S(1)} %shard_map.111), channel_id=1, source_target_pairs={{0,4},{4,0},{1,5},{5,1},{2,6},{6,2},{3,7},{7,3},{8,12},{12,8},{9,1... | collective-permute-start | bytes 36872 | tf_op jit(solution)/shard_map/ppermute | solution.py:604
  25.2 2.2 %collective-permute-done.4 = f32[24,128]{1,0:T(8,128)S(1)} collective-permute-done((f32[24,128]{1,0:T(8,128)S(1)}, f32[24,128]{1,0:T(8,128)S(1)}, u32[]{:S(2)}, u32[]{:S(2)}) %collective-permute-start.4) | collective-permute-done | bytes 12320 | tf_op jit(solution)/shard_map/ppermute | solution.py:604
  27.4 0.0 collective-permute-start.5
  27.4 1.2 %collective-permute-done.5 = f32[24,128]{1,0:T(8,128)S(1)} collective-permute-done((f32[24,128]{1,0:T(8,128)S(1)}, f32[24,128]{1,0:T(8,128)S(1)}, u32[]{:S(2)}, u32[]{:S(2)}) %collective-permute-start.5) | collective-permute-done | bytes 12320 | tf_op jit(solution)/shard_map/ppermute | solution.py:604
  28.6 1.5 %collective-permute-start.6 = (f32[24,128]{1,0:T(8,128)S(1)}, f32[24,128]{1,0:T(8,128)S(1)}, u32[]{:S(2)}, u32[]{:S(2)}) collective-permute-start(f32[24,128]{1,0:T(8,128)S(1)} %add.13), channel_id=1, source_target_pairs={{0,16},{8,24},{16,0},{24,8},{1,17},{9,25},{17,1},{25,9},{2,18},{10... | collective-permute-start | bytes 36872 | tf_op jit(solution)/shard_map/ppermute | solution.py:604
  30.1 2.2 %collective-permute-done.6 = f32[24,128]{1,0:T(8,128)S(1)} collective-permute-done((f32[24,128]{1,0:T(8,128)S(1)}, f32[24,128]{1,0:T(8,128)S(1)}, u32[]{:S(2)}, u32[]{:S(2)}) %collective-permute-start.6) | collective-permute-done | bytes 12320 | tf_op jit(solution)/shard_map/ppermute | solution.py:604
  32.3 0.0 collective-permute-start.7
  32.3 3.7 %collective-permute-done.7 = f32[24,128]{1,0:T(8,128)S(1)} collective-permute-done((f32[24,128]{1,0:T(8,128)S(1)}, f32[24,128]{1,0:T(8,128)S(1)}, u32[]{:S(2)}, u32[]{:S(2)}) %collective-permute-start.7) | collective-permute-done | bytes 12320 | tf_op jit(solution)/shard_map/ppermute | solution.py:604
  36.0 0.2 collective-permute-start.8
  36.2 4.4 %collective-permute-done.8.gram_b = f32[24,128]{1,0:T(8,128)S(1)} collective-permute-done((f32[24,128]{1,0:T(8,128)S(1)}, f32[24,128]{1,0:T(8,128)S(1)}, u32[]{:S(2)}, u32[]{:S(2)}) %collective-permute-start.8) | collective-permute-done | bytes 12320 | tf_op jit(solution)/shard_map/ppermute | solution.py:604
  40.6 2.2 %shard_map.112 = f32[4,4,24]{2,1,0:T(4,128)} custom-call(f32[24,128]{1,0:T(8,128)S(1)} %add.15.gram_a, f32[24,128]{1,0:T(8,128)S(1)} %collective-permute-done.8.gram_b, f32[16,8,24]{2,1,0:T(8,128)S(1)} %get-tuple-element.20.theta_ref), custom_call_target="tpu_custom_call" | custom-call | flops 2200000000 | bytes 7000000 | tf_op jit(solution)/shard_map/pallas_call | solution.py:607
  (4 shorter events, 0.0 us)
Async XLA Ops:
  0.0 9.4 %collective-permute-start = (f32[4,8,24]{2,1,0:T(8,128)}, f32[4,8,24]{2,1,0:T(8,128)S(1)}, u32[]{:S(2)}, u32[]{:S(2)}) collective-permute-start(f32[4,8,24]{2,1,0:T(8,128)} %refs_4_.1), channel_id=1, source_target_pairs={{0,1},{1,0},{2,3},{3,2},{4,5},{5,4},{6,7},{7,6},{8,9},{9,8},{10,11... | collective-permute-start | bytes 9224 | tf_op jit(solution)/shard_map/ppermute | solution.py:551
  3.0 6.4 %collective-permute-start.1 = (f32[4,8,24]{2,1,0:T(8,128)}, f32[4,8,24]{2,1,0:T(8,128)S(1)}, u32[]{:S(2)}, u32[]{:S(2)}) collective-permute-start(f32[4,8,24]{2,1,0:T(8,128)} %refs_4_.1), channel_id=1, source_target_pairs={{0,2},{1,3},{2,0},{3,1},{4,6},{5,7},{6,4},{7,5},{8,10},{9,11},{10,... | collective-permute-start | bytes 9224 | tf_op jit(solution)/shard_map/ppermute | solution.py:551
  5.6 5.7 %collective-permute-start.2 = (f32[4,8,24]{2,1,0:T(8,128)}, f32[4,8,24]{2,1,0:T(8,128)S(1)}, u32[]{:S(2)}, u32[]{:S(2)}) collective-permute-start(f32[4,8,24]{2,1,0:T(8,128)} %refs_4_.1), channel_id=1, source_target_pairs={{0,3},{1,2},{2,1},{3,0},{4,7},{5,6},{6,5},{7,4},{8,11},{9,10},{10,... | collective-permute-start | bytes 9224 | tf_op jit(solution)/shard_map/ppermute | solution.py:551
  7.6 9.5 %collective-permute-start.3 = (bf16[160,384]{1,0:T(8,128)(2,1)S(1)}, bf16[160,384]{1,0:T(8,128)(2,1)S(1)}, u32[]{:S(2)}, u32[]{:S(2)}) collective-permute-start(bf16[160,384]{1,0:T(8,128)(2,1)S(1)} %get-tuple-element.16.refs_1_), channel_id=1, source_target_pairs={{0,4},{4,0},{1,5},{5,1},{2,6},{6,2},{3,7},{7,3},{8,12},{12,8},{9,1... | collective-permute-start | bytes 368648 | tf_op jit(solution)/shard_map/ppermute | solution.py:541
  23.7 3.7 %collective-permute-start.4 = (f32[24,128]{1,0:T(8,128)S(1)}, f32[24,128]{1,0:T(8,128)S(1)}, u32[]{:S(2)}, u32[]{:S(2)}) collective-permute-start(f32[24,128]{1,0:T(8,128)S(1)} %shard_map.111), channel_id=1, source_target_pairs={{0,4},{4,0},{1,5},{5,1},{2,6},{6,2},{3,7},{7,3},{8,12},{12,8},{9,1... | collective-permute-start | bytes 36872 | tf_op jit(solution)/shard_map/ppermute | solution.py:604
  27.4 1.2 %collective-permute-start.5 = (f32[24,128]{1,0:T(8,128)S(1)}, f32[24,128]{1,0:T(8,128)S(1)}, u32[]{:S(2)}, u32[]{:S(2)}) collective-permute-start(f32[24,128]{1,0:T(8,128)S(1)} %add.12), channel_id=1, source_target_pairs={{0,8},{8,0},{16,24},{24,16},{1,9},{9,1},{17,25},{25,17},{2,10},{10... | collective-permute-start | bytes 36872 | tf_op jit(solution)/shard_map/ppermute | solution.py:604
  28.6 3.7 %collective-permute-start.6 = (f32[24,128]{1,0:T(8,128)S(1)}, f32[24,128]{1,0:T(8,128)S(1)}, u32[]{:S(2)}, u32[]{:S(2)}) collective-permute-start(f32[24,128]{1,0:T(8,128)S(1)} %add.13), channel_id=1, source_target_pairs={{0,16},{8,24},{16,0},{24,8},{1,17},{9,25},{17,1},{25,9},{2,18},{10... | collective-permute-start | bytes 36872 | tf_op jit(solution)/shard_map/ppermute | solution.py:604
  32.3 3.7 %collective-permute-start.7 = (f32[24,128]{1,0:T(8,128)S(1)}, f32[24,128]{1,0:T(8,128)S(1)}, u32[]{:S(2)}, u32[]{:S(2)}) collective-permute-start(f32[24,128]{1,0:T(8,128)S(1)} %add.14), channel_id=1, source_target_pairs={{0,1},{1,0},{2,3},{3,2},{4,5},{5,4},{6,7},{7,6},{8,9},{9,8},{10,11... | collective-permute-start | bytes 36872 | tf_op jit(solution)/shard_map/ppermute | solution.py:604
  36.0 4.6 %collective-permute-start.8 = (f32[24,128]{1,0:T(8,128)S(1)}, f32[24,128]{1,0:T(8,128)S(1)}, u32[]{:S(2)}, u32[]{:S(2)}) collective-permute-start(f32[24,128]{1,0:T(8,128)S(1)} %add.15.gram_a), channel_id=1, source_target_pairs={{0,2},{1,3},{2,0},{3,1},{4,6},{5,7},{6,4},{7,5},{8,10},{9,11},{10,... | collective-permute-start | bytes 36872 | tf_op jit(solution)/shard_map/ppermute | solution.py:604

commit v3 on v2

--- a/solution.py
+++ b/solution.py
@@ -14,7 +14,7 @@
 LANES = 2 * SLOTS
 ALPHA_INFLATION = 4.0
 GROUP = 4
-BLOCK = 4
+TURN = 24
 VMEM_LIMIT = 48 * 2**20
 F32 = jnp.float32
 BF16 = jnp.bfloat16
@@ -113,6 +113,7 @@
         axis=0,
     ).astype(BF16)
     out_ref[:, pl.ds(width, 2 * channels)] = lhs
+    win = win[:, forcing:]
     win_pad = jnp.zeros((block - channels, win.shape[1]), F32)
     out_ref[:, pl.ds(width + 128, win.shape[1])] = jnp.concatenate([win, win_pad], axis=0).astype(
         BF16
@@ -121,8 +122,8 @@
 
 def prepare(plan, *refs):
     sources, refs = refs[:11], refs[11:]
-    folded, theta, x, y, w = refs[:5]
-    buffers, (quad, stack, sems) = refs[5:15], refs[15:]
+    folded, theta, x, y, w, pred = refs[:6]
+    buffers, (quad, stack, sems, spread), scratch = refs[6:16], refs[16:20], refs[20:]
     mine = lax.axis_index("member") // plan[2]
     sliced = [s.at[mine] if i < 3 else s for i, s in enumerate(sources)]
     copies = list(zip(sliced, buffers[:4] + (theta,) + buffers[4:]))
@@ -130,6 +131,19 @@
     fetch(copies, sems)()
     fold_weights(mine, *buffers[:4], folded, quad, stack)
     pack_slots(plan, *buffers[4:], x, y, w)
+    own = pred.shape[1]
+    spread_block(lambda i, r: theta[i, pl.ds(r, 1), :], own, spread, 0)
+    run_crop(x, 0, folded, spread, 0, own, lambda i: i, pred, *scratch)
+
+
+def spread_block(row_of, count, spread, at):
+    for i in range(count):
+        for half in range(2):
+            for r in range(REGIONS):
+                row = row_of(i + half * count, r)
+                spread[pl.ds((at + i) * LANES + half * SLOTS + r * CAP, CAP), :] = (
+                    jnp.broadcast_to(row, (CAP, row.shape[1]))
+                )
 
 
 def pack_slots(
@@ -222,41 +236,52 @@
     return lax.axis_size("crop")
 
 
-def net_first(dims, *refs):
-    blocks_in, n_forcing = dims
-    x_ref, wts = refs[:2]
-    theta_refs, refs = refs[2 : 2 + blocks_in], refs[2 + blocks_in :]
+def other_member(d):
+    me, count = lax.axis_index("member"), lax.axis_size("member")
+    return me ^ d if count in (2, 4) else lax.rem(me + d, count)
+
+
+def pair_row(i, own):
+    return other_member(lax.div(i, own)) * own + lax.rem(i, own)
+
+
+def net_first(blocks_in, *refs):
+    x_ref, wts, pred_own, theta_own = refs[:4]
+    theta_refs, refs = refs[4 : 4 + blocks_in], refs[4 + blocks_in :]
     pred, theta_out, spread = refs[:3]
-    theta_all = refs[3]
-    scratch = refs[4:]
-    members, _, n_params = theta_out.shape
-    pairs = members // 2
+    scratch = refs[3:]
+    block = theta_own.shape[0]
+    own = block // 2
+    shards = theta_out.shape[0] // block
+    weeks, pairs = pred.shape[0], pred.shape[1]
     me = lax.axis_index("member")
 
-    theta_all[...] = jnp.zeros(theta_all.shape, F32)
-    for d, ref in enumerate(theta_refs):
-        count = ref.shape[0]
-        at = (me ^ d) * count if blocks_in > 1 else 0
-        for i in range(count):
-            theta_all[at + i, :, pl.ds(n_forcing, n_params)] = ref[i]
-            theta_out[at + i] = ref[i]
-
-    for i in range(pairs):
-        for half in range(2):
-            for r in range(REGIONS):
-                row = theta_all[i + half * pairs, pl.ds(r, 1), :]
-                spread[pl.ds(i * LANES + half * SLOTS + r * CAP, CAP), :] = jnp.broadcast_to(
-                    row, (CAP, row.shape[1])
-                )
-    run_crop(x_ref, 0, wts, spread, pred, *scratch)
-
-
-def run_crop(x_ref, n, wts, spread, pred, base, inner0, inner1, bias_full, bias_now):
+    for i in range(block):
+        theta_out[me * block + i] = theta_own[i]
+    spread_block(lambda i, r: theta_own[i, pl.ds(r, 1), :], own, spread, 0)
+    for d in range(1, shards):
+        if blocks_in == 1 and shards > 2:
+            ref, at = theta_refs[0], other_member(d) * block
+        else:
+            ref, at = theta_refs[d - 1], 0
+        for i in range(block):
+            theta_out[other_member(d) * block + i] = ref[at + i]
+        spread_block(lambda i, r: ref[at + i, pl.ds(r, 1), :], own, spread, d * own)
+    for t in range(weeks):
+        for i in range(own):
+            pred[t, pl.ds(me * own + i, 1), :] = pred_own[t, pl.ds(i, 1), :]
+    run_crop(
+        x_ref, 0, wts, spread, own, pairs - own, lambda i: pair_row(i + own, own), pred, *scratch
+    )
+
+
+def run_crop(
+    x_ref, n, wts, spread, start, pairs, row_of, pred, base, inner0, inner1, bias_full, bias_now
+):
     layers, n_forcing = x_ref.shape[1], x_ref.shape[2] // 2
     channels = base.shape[0]
     taps, block = weight_rows(layers, channels)
     width = 2 * n_forcing + 2 * (layers - 1) * channels
-    pairs = pred.shape[1]
     tiles = pred.shape[0] // 2
     span = 2 * LANES
 
@@ -266,7 +291,8 @@
     stack = wts[:, pl.ds(width, 2 * channels)]
     now = stack[:taps, :channels]
     win = wts[pl.ds(0, channels), pl.ds(width + 128, spread.shape[1])]
-    high, low = hi_lo(mm_nt(win, spread[...].astype(BF16)))
+    theta_rows = spread[pl.ds(start * LANES, pairs * LANES), :].astype(BF16)
+    high, low = hi_lo(mm_nt(win, theta_rows))
     bias_full[...] = mm(
         jnp.concatenate([stack, stack], axis=1),
         jnp.concatenate([high, high, low, low], axis=0),
@@ -288,10 +314,12 @@
     zero_tile = jnp.zeros((channels, span), BF16)
 
     group = inner0.shape[0]
+    length = TURN // group
 
     @pl.loop(0, pairs // group)
     def _(step):
         items = [step * group + u for u in range(group)]
+        rows_out = [row_of(i) for i in items]
         lanes = [pl.ds(pl.multiple_of(i * LANES, LANES), LANES) for i in items]
 
         def bias_of(u, layer):
@@ -348,10 +376,10 @@
                     + v[channels + 1 : channels + 2]
                     + jnp.concatenate([head_bias, head_bias], axis=1)
                 )
-                pred[2 * j, pl.ds(items[u], 1), :] = s[:, :LANES]
-                pred[2 * j + 1, pl.ds(items[u], 1), :] = s[:, LANES:]
-
-        blocks = [range(j, min(j + BLOCK, tiles)) for j in range(0, tiles, BLOCK)]
+                pred[2 * j, pl.ds(rows_out[u], 1), :] = s[:, :LANES]
+                pred[2 * j + 1, pl.ds(rows_out[u], 1), :] = s[:, LANES:]
+
+        blocks = [range(j, min(j + length, tiles)) for j in range(0, tiles, length)]
         for step_at in range(len(blocks) + 2):
             if step_at < len(blocks):
                 layer0(blocks[step_at])
@@ -362,14 +390,16 @@
                     layer2(u, blocks[step_at - 2])
 
 
-def net_last(n_crops, *refs):
+def net_last(n_crops, own, *refs):
     x_ref, y_ref, w_ref, pred_first = refs[:4]
     refs = refs[4:]
     preds = [pred_first]
     if n_crops == 2:
         wts, spread = refs[:2]
         out_ref, pred = refs[2:4]
-        run_crop(x_ref, 1, wts, spread, pred, *refs[4:])
+        run_crop(
+            x_ref, 1, wts, spread, 0, pred.shape[1], lambda i: pair_row(i, own), pred, *refs[4:]
+        )
         preds.append(pred)
     else:
         out_ref = refs[0]
@@ -418,11 +448,13 @@
     out_ref[...] = flat[: members + 8]
 
 
-def solve_kernel(owned, gram_a, gram_b, theta_ref, out_ref, system, moved):
+def solve_kernel(owned, gram_a, gram_b, theta_ref, out_ref, system, moved, joint):
     members, _, n_params = theta_ref.shape
     my_members = out_ref.shape[0]
+    own, pairs = my_members // 2, members // 2
+    order = [p // own * my_members + p % own + half * own for half in range(2) for p in range(pairs)]
     first_region = lax.axis_index("crop") * owned
-    first_member = lax.axis_index("member") * my_members
+    first_pair = lax.axis_index("member") * own
     gram = gram_a[...] + gram_b[...]
     for r in range(REGIONS):
         system[r] = gram[:, r * members : (r + 1) * members]
@@ -431,33 +463,45 @@
         jnp.int32, (members, members), 1
     )
     scale_root = math.sqrt(members - 1)
+    joint[...] = jnp.zeros(joint.shape, F32)
     work = []
     for k in range(owned):
         block = system[first_region + k]
         g = block[:members]
         proj = block[members : members + 1] + block[members + 1 : members + 2]
         theta = jnp.concatenate(
-            [theta_ref[m, pl.ds(first_region + k, 1), :] for m in range(members)], axis=0
+            [theta_ref[m, pl.ds(first_region + k, 1), :] for m in order], axis=0
         )
         spread = (theta - jnp.sum(theta, axis=0, keepdims=True) / members) / scale_root
-        work.append([g + jnp.where(eye, 1.0, 0.0), spread, proj - scale_root * g, theta])
-    for i in range(members):
-        for item in work:
-            a, z = item[0], item[1]
-            column = a[:, i : i + 1]
-            pivot = a[i : i + 1, i : i + 1]
-            row_a = a[i : i + 1] / pivot
-            row_z = z[i : i + 1] / pivot
-            factor = jnp.where(row_id == i, column - 1.0, column)
-            item[0] = a - factor * row_a
-            item[1] = z - factor * row_z
-    for k, (_, z, right, theta) in enumerate(work):
+        joint[k, :, pl.ds(0, members)] = g + jnp.where(eye, 1.0, 0.0)
+        joint[k, :, pl.ds(members, n_params)] = spread
+        work.append((proj - scale_root * g, theta))
+    both = [joint[k] for k in range(owned)]
+    width = joint.shape[2]
+    for i in range(0, members, 2):
+        for k, a in enumerate(both):
+            col0 = jnp.broadcast_to(a[:, i : i + 1], (members, width))
+            col1 = jnp.broadcast_to(a[:, i + 1 : i + 2], (members, width))
+            inv0 = 1.0 / col0[i : i + 1]
+            row0 = a[i : i + 1] * inv0
+            below = col0[i + 1 : i + 2]
+            ahead = col1[i : i + 1] * inv0
+            inv1 = 1.0 / (col1[i + 1 : i + 2] - below * ahead)
+            row1 = (a[i + 1 : i + 2] - below * row0) * inv1
+            row0 = row0 - ahead * row1
+            col0 = jnp.where(row_id == i, col0 - 1.0, col0)
+            col1 = jnp.where(row_id == i + 1, col1 - 1.0, col1)
+            both[k] = a - col0 * row0 - col1 * row1
+    for k, (right, theta) in enumerate(work):
+        joint[k] = both[k]
+        z = joint[k, :, pl.ds(members, n_params)]
         moved[k] = theta + jnp.dot(
             right, z, precision=lax.Precision.HIGHEST, preferred_element_type=F32
         )
     for k in range(owned):
         for m in range(my_members):
-            out_ref[m, pl.ds(k, 1), :] = moved[k, pl.ds(first_member + m, 1), :]
+            row = first_pair + m // own * pairs + m % own
+            out_ref[m, pl.ds(k, 1), :] = moved[k, pl.ds(row, 1), :]
 
 
 def local(
@@ -492,8 +536,20 @@
     wide = -(-(width + 128 + n_forcing + n_params) // 128) * 128
     vmem_copy = lambda a: pltpu.VMEM(a.shape[1:], a.dtype)
 
+    own, pairs = my_members // 2, members // 2
+
+    def scratch(count):
+        group = max(g for g in range(1, GROUP + 1) if count % g == 0)
+        return [
+            pltpu.VMEM((channels, weeks * LANES), F32),
+            pltpu.VMEM((group, channels, weeks * LANES), BF16),
+            pltpu.VMEM((group, channels, weeks * LANES), BF16),
+            pltpu.VMEM((block, count * LANES), F32),
+            pltpu.VMEM((taps, count * LANES), F32),
+        ]
+
     input_rows = jnp.swapaxes(input_weight, 1, 2)
-    folded, theta_own, x, y, w = pl.pallas_call(
+    folded, theta_own, x, y, w, pred_own = pl.pallas_call(
         functools.partial(prepare, plan),
         out_shape=(
             jax.ShapeDtypeStruct((block, wide), BF16),
@@ -501,9 +557,10 @@
             jax.ShapeDtypeStruct((n_crops, layers, 2 * n_forcing, weeks * LANES), BF16),
             jax.ShapeDtypeStruct((n_crops, weeks, LANES), F32),
             jax.ShapeDtypeStruct((n_crops, weeks, LANES), F32),
+            jax.ShapeDtypeStruct((weeks, own, LANES), F32),
         ),
         in_specs=hbm(11),
-        out_specs=tuple(vmem(5)),
+        out_specs=tuple(vmem(6)),
         scratch_shapes=[
             vmem_copy(input_rows),
             vmem_copy(conv_weight),
@@ -518,9 +575,11 @@
             pltpu.VMEM((2 * channels, width), F32),
             pltpu.VMEM((block, 128), F32),
             pltpu.SemaphoreType.DMA((11,)),
-        ],
+            pltpu.VMEM((own * LANES, n_params), F32),
+        ]
+        + scratch(own),
         compiler_params=params_kernel,
-        cost_estimate=cost(2),
+        cost_estimate=cost(4),
     )(
         *stay(
             input_rows,
@@ -547,47 +606,39 @@
             for n in range(n_crops)
         ]
     if n_member in (2, 4):
-        thetas = [theta_own] + [
+        thetas = [
             lax.ppermute(params, "member", [(i, i ^ d) for i in range(n_member)])
             for d in range(1, n_member)
         ]
     else:
         thetas = [lax.all_gather(params, "member", axis=0, tiled=True)]
 
-    pairs = members // 2
-    group = math.gcd(pairs, GROUP)
-    scratch = [
-        pltpu.VMEM((channels, weeks * LANES), F32),
-        pltpu.VMEM((group, channels, weeks * LANES), BF16),
-        pltpu.VMEM((group, channels, weeks * LANES), BF16),
-        pltpu.VMEM((block, pairs * LANES), F32),
-        pltpu.VMEM((taps, pairs * LANES), F32),
-    ]
     pred, theta_all, spread = pl.pallas_call(
-        functools.partial(net_first, (len(thetas), n_forcing)),
+        functools.partial(net_first, len(thetas)),
         out_shape=(
             jax.ShapeDtypeStruct((weeks, pairs, LANES), F32),
             jax.ShapeDtypeStruct((members, REGIONS, n_params), F32),
-            jax.ShapeDtypeStruct((pairs * LANES, n_forcing + n_params), F32),
+            jax.ShapeDtypeStruct((pairs * LANES, n_params), F32),
         ),
-        in_specs=vmem(2 + len(thetas)),
+        in_specs=vmem(4 + len(thetas)),
         out_specs=tuple(vmem(3)),
-        scratch_shapes=[pltpu.VMEM((members, REGIONS, n_forcing + n_params), F32)] + scratch,
+        scratch_shapes=scratch(pairs - own),
         compiler_params=params_kernel,
-        cost_estimate=cost(7),
-    )(x, weights[0], *thetas)
+        cost_estimate=cost(5),
+    )(x, weights[0], pred_own, theta_own, *thetas)
     rest = [x, y, w, pred]
-    scratch = [pltpu.VMEM((weeks, pairs, LANES), F32)] + scratch
+    held = []
     if n_crops == 2:
         rest += [weights[1], spread]
+        held = [pltpu.VMEM((weeks, pairs, LANES), F32)] + scratch(pairs)
     gram = pl.pallas_call(
-        functools.partial(net_last, n_crops),
+        functools.partial(net_last, n_crops, own),
         out_shape=jax.ShapeDtypeStruct((members + 8, REGIONS * members), F32),
         in_specs=vmem(len(rest)),
         out_specs=vmem(1)[0],
-        scratch_shapes=scratch if n_crops == 2 else [],
+        scratch_shapes=held,
         compiler_params=params_kernel,
-        cost_estimate=cost(8),
+        cost_estimate=cost(7),
     )(*rest)
 
     steps = []
@@ -612,6 +663,7 @@
         scratch_shapes=[
             pltpu.VMEM((REGIONS, members + 8, members), F32),
             pltpu.VMEM((owned, members, n_params), F32),
+            pltpu.VMEM((owned, members, -(-(members + n_params) // 128) * 128), F32),
         ],
         compiler_params=params_kernel,
         cost_estimate=cost(2),

time: 43 us -> 41.6 us (0.967)
  waiting for transfers between devices: 15.6 us -> 12.1 us
  starting transfers between devices: 10.6 us -> 12.5 us
    ppermute x5, waiting for transfers between devices: 13.6 us -> 11.8 us  [local(): other = lax.ppermute(gram, axis, pairs_)]
    ppermute x5, starting transfers between devices: 3.27 us -> 5.14 us  [local(): other = lax.ppermute(gram, axis, pairs_)]
    ppermute x3, waiting for transfers between devices: 1.97 us -> 0.38 us  [local(): lax.ppermute(params, 'member', [(i, i ^ d) for i in range(n_member)])]
    pallas_call x1, Pallas kernels: 2 us -> 3.58 us  [local(): pl.pallas_call(functools.partial(prepare, plan), out_shape=(jax.ShapeDtyp...]
    pallas_call x2, Pallas kernels: 12.3 us -> 11.3 us  [the longest x1 6.75 us: local(): pl.pallas_call(functools.partial(net_last, n_crops, own), out_shape=jax.S...]
  transfers between devices with their start and end apart: 9 -> 9, of which waited for: 6 -> 6; matrix products, arithmetic and copies ran while one was open for 0% -> 0% of each run, Pallas kernels for 18% -> 20%
where the time goes in v3:
time: 41.6 us; the launch traced here: 41.4 us
  Pallas kernels  16.7 us (40%)
  starting transfers between devices  12.5 us (30%)
  waiting for transfers between devices  12.1 us (29%)
    ppermute x5, waiting for transfers between devices, local(): other = lax.ppermute(gram, axis, pairs_)  11.8 us
    pallas_call x1, Pallas kernels, local(): pl.pallas_call(functools.partial(net_last, n_crops, own), out_shape=jax.S...  6.75 us
    ppermute x3, starting transfers between devices, local(): lax.ppermute(params, 'member', [(i, i ^ d) for i in range(n_member)])  5.62 us
    ppermute x5, starting transfers between devices, local(): other = lax.ppermute(gram, axis, pairs_)  5.14 us
    pallas_call x1, Pallas kernels, local(): pl.pallas_call(functools.partial(net_first, len(thetas)), out_shape=(jax....  4.57 us
    pallas_call x1, Pallas kernels, local(): pl.pallas_call(functools.partial(prepare, plan), out_shape=(jax.ShapeDtyp...  3.58 us
    pallas_call x1, Pallas kernels, local(): pl.pallas_call(functools.partial(solve_kernel, owned), out_shape=jax.Shap...  1.82 us
    ppermute x1, starting transfers between devices, local(): weights = [folded, lax.ppermute(folded, 'crop', [(0, 1), (1, 0)])]  1.77 us
  transfers between devices with their start and end apart: 9, of which 6 were waited for; matrix products, arithmetic and copies ran while one was open for 0% of the time, Pallas kernels for 20%

profile of v3, /device:TPU:0, one launch (start us, length us, event | category | flops | bytes accessed | tf_op | source)
XLA Modules:
  0.0 41.4 jit_solution(14871996621584473305)
XLA Ops:
  0.0 3.0 %collective-permute-start = (f32[4,8,24]{2,1,0:T(8,128)}, f32[4,8,24]{2,1,0:T(8,128)S(1)}, u32[]{:S(2)}, u32[]{:S(2)}) collective-permute-start(f32[4,8,24]{2,1,0:T(8,128)} %refs_4_.1), channel_id=1, source_target_pairs={{0,1},{1,0},{2,3},{3,2},{4,5},{5,4},{6,7},{7,6},{8,9},{9,8},{10,11... | collective-permute-start | bytes 9224 | tf_op jit(solution)/shard_map/ppermute | solution.py:610
  3.0 2.6 %collective-permute-start.1 = (f32[4,8,24]{2,1,0:T(8,128)}, f32[4,8,24]{2,1,0:T(8,128)S(1)}, u32[]{:S(2)}, u32[]{:S(2)}) collective-permute-start(f32[4,8,24]{2,1,0:T(8,128)} %refs_4_.1), channel_id=1, source_target_pairs={{0,2},{1,3},{2,0},{3,1},{4,6},{5,7},{6,4},{7,5},{8,10},{9,11},{10,... | collective-permute-start | bytes 9224 | tf_op jit(solution)/shard_map/ppermute | solution.py:610
  5.6 0.0 collective-permute-start.2
  5.6 3.6 %shard_map.109 = (bf16[160,384]{1,0:T(8,128)(2,1)S(1)}, f32[4,8,24]{2,1,0:T(8,128)S(1)}, bf16[2,3,16,6656]{3,2,1,0:T(8,128)(2,1)S(1)}, f32[2,52,128]{2,1,0:T(8,1...) custom-call(bf16[4,32,48]{2,1,0:T(8,128)(2,1)} %bitcast.4, bf16[4,3,48,96]{3,2,1,0:T(8,128)(2,1)} %refs_1_.1, ...), custom_call_target="tpu_custom_call" | custom-call | flops 4400000000 | bytes 14000000 | tf_op jit(solution)/shard_map/pallas_call | solution.py:552
  9.2 1.8 %collective-permute-start.3 = (bf16[160,384]{1,0:T(8,128)(2,1)S(1)}, bf16[160,384]{1,0:T(8,128)(2,1)S(1)}, u32[]{:S(2)}, u32[]{:S(2)}) collective-permute-start(bf16[160,384]{1,0:T(8,128)(2,1)S(1)} %get-tuple-element.17.refs_1_), channel_id=1, source_target_pairs={{0,4},{4,0},{1,5},{5,1},{2,6},{6,2},{3,7},{7,3},{8,12},{12,8},{9,1... | collective-permute-start | bytes 368648 | tf_op jit(solution)/shard_map/ppermute | solution.py:600
  11.0 0.0 collective-permute-done.refs_4_
  11.0 0.0 collective-permute-done.1.refs_5_
  11.0 0.4 collective-permute-done.2.refs_6_
  11.4 4.6 %shard_map.110 = (f32[52,8,128]{2,1,0:T(8,128)S(1)}, f32[16,8,24]{2,1,0:T(8,128)S(1)}, f32[1024,24]{1,0:T(8,128)S(1)}) custom-call(bf16[2,3,16,6656]{3,2,1,0:T(8,128)(2,1)S(1)} %get-tuple-element.14.refs_0_, bf16[160,384]{1,0:T(8,128)(2,1)S(1)} %get-tuple-element.17.refs_1_, f32[52,2,128]{2,1,0:T(2,128)S(1)} %get-tuple-element.18.refs_2_, ...), custom_call_target="tpu_custom_call" | custom-call | flops 5500000256 | bytes 17500000 | tf_op jit(solution)/shard_map/pallas_call | solution.py:616
  15.9 0.0 collective-permute-done.3.refs_4_
  15.9 6.8 %shard_map.111 = f32[24,128]{1,0:T(8,128)S(1)} custom-call(bf16[2,3,16,6656]{3,2,1,0:T(8,128)(2,1)S(1)} %get-tuple-element.14.refs_0_, f32[2,52,128]{2,1,0:T(8,128)S(1)} %get-tuple-element.15.refs_1_, f32[2,52,128]{2,1,0:T(8,128)S(1)} %get-tuple-element.16.refs_2_, f32[52,8,128]{2,1,0:T(8,128)S(1)} %get-tuple-element.20.refs_3_, ...), custom_call_target="tpu_custom_call" | custom-call | flops 7699999744 | bytes 24500000 | tf_op jit(solution)/shard_map/pallas_call | solution.py:634
  22.7 1.5 %collective-permute-start.4 = (f32[24,128]{1,0:T(8,128)S(1)}, f32[24,128]{1,0:T(8,128)S(1)}, u32[]{:S(2)}, u32[]{:S(2)}) collective-permute-start(f32[24,128]{1,0:T(8,128)S(1)} %shard_map.111), channel_id=1, source_target_pairs={{0,4},{4,0},{1,5},{5,1},{2,6},{6,2},{3,7},{7,3},{8,12},{12,8},{9,1... | collective-permute-start | bytes 36872 | tf_op jit(solution)/shard_map/ppermute | solution.py:655
  24.2 2.2 %collective-permute-done.4 = f32[24,128]{1,0:T(8,128)S(1)} collective-permute-done((f32[24,128]{1,0:T(8,128)S(1)}, f32[24,128]{1,0:T(8,128)S(1)}, u32[]{:S(2)}, u32[]{:S(2)}) %collective-permute-start.4) | collective-permute-done | bytes 12320 | tf_op jit(solution)/shard_map/ppermute | solution.py:655
  26.4 0.0 collective-permute-start.5
  26.4 1.2 %collective-permute-done.5 = f32[24,128]{1,0:T(8,128)S(1)} collective-permute-done((f32[24,128]{1,0:T(8,128)S(1)}, f32[24,128]{1,0:T(8,128)S(1)}, u32[]{:S(2)}, u32[]{:S(2)}) %collective-permute-start.5) | collective-permute-done | bytes 12320 | tf_op jit(solution)/shard_map/ppermute | solution.py:655
  27.6 1.5 %collective-permute-start.6 = (f32[24,128]{1,0:T(8,128)S(1)}, f32[24,128]{1,0:T(8,128)S(1)}, u32[]{:S(2)}, u32[]{:S(2)}) collective-permute-start(f32[24,128]{1,0:T(8,128)S(1)} %add.13), channel_id=1, source_target_pairs={{0,16},{8,24},{16,0},{24,8},{1,17},{9,25},{17,1},{25,9},{2,18},{10... | collective-permute-start | bytes 36872 | tf_op jit(solution)/shard_map/ppermute | solution.py:655
  29.1 2.2 %collective-permute-done.6 = f32[24,128]{1,0:T(8,128)S(1)} collective-permute-done((f32[24,128]{1,0:T(8,128)S(1)}, f32[24,128]{1,0:T(8,128)S(1)}, u32[]{:S(2)}, u32[]{:S(2)}) %collective-permute-start.6) | collective-permute-done | bytes 12320 | tf_op jit(solution)/shard_map/ppermute | solution.py:655
  31.3 0.3 collective-permute-start.7
  31.6 3.4 %collective-permute-done.7 = f32[24,128]{1,0:T(8,128)S(1)} collective-permute-done((f32[24,128]{1,0:T(8,128)S(1)}, f32[24,128]{1,0:T(8,128)S(1)}, u32[]{:S(2)}, u32[]{:S(2)}) %collective-permute-start.7) | collective-permute-done | bytes 12320 | tf_op jit(solution)/shard_map/ppermute | solution.py:655
  35.0 1.8 %collective-permute-start.8 = (f32[24,128]{1,0:T(8,128)S(1)}, f32[24,128]{1,0:T(8,128)S(1)}, u32[]{:S(2)}, u32[]{:S(2)}) collective-permute-start(f32[24,128]{1,0:T(8,128)S(1)} %add.15.gram_a), channel_id=1, source_target_pairs={{0,2},{1,3},{2,0},{3,1},{4,6},{5,7},{6,4},{7,5},{8,10},{9,11},{10,... | collective-permute-start | bytes 36872 | tf_op jit(solution)/shard_map/ppermute | solution.py:655
  36.8 2.8 %collective-permute-done.8.gram_b = f32[24,128]{1,0:T(8,128)S(1)} collective-permute-done((f32[24,128]{1,0:T(8,128)S(1)}, f32[24,128]{1,0:T(8,128)S(1)}, u32[]{:S(2)}, u32[]{:S(2)}) %collective-permute-start.8) | collective-permute-done | bytes 12320 | tf_op jit(solution)/shard_map/ppermute | solution.py:655
  39.6 1.8 %shard_map.112 = f32[4,4,24]{2,1,0:T(4,128)} custom-call(f32[24,128]{1,0:T(8,128)S(1)} %add.15.gram_a, f32[24,128]{1,0:T(8,128)S(1)} %collective-permute-done.8.gram_b, f32[16,8,24]{2,1,0:T(8,128)S(1)} %get-tuple-element.22.theta_ref), custom_call_target="tpu_custom_call" | custom-call | flops 2200000000 | bytes 7000000 | tf_op jit(solution)/shard_map/pallas_call | solution.py:658
  (4 shorter events, 0.0 us)
Async XLA Ops:
  0.0 11.0 %collective-permute-start = (f32[4,8,24]{2,1,0:T(8,128)}, f32[4,8,24]{2,1,0:T(8,128)S(1)}, u32[]{:S(2)}, u32[]{:S(2)}) collective-permute-start(f32[4,8,24]{2,1,0:T(8,128)} %refs_4_.1), channel_id=1, source_target_pairs={{0,1},{1,0},{2,3},{3,2},{4,5},{5,4},{6,7},{7,6},{8,9},{9,8},{10,11... | collective-permute-start | bytes 9224 | tf_op jit(solution)/shard_map/ppermute | solution.py:610
  3.0 8.0 %collective-permute-start.1 = (f32[4,8,24]{2,1,0:T(8,128)}, f32[4,8,24]{2,1,0:T(8,128)S(1)}, u32[]{:S(2)}, u32[]{:S(2)}) collective-permute-start(f32[4,8,24]{2,1,0:T(8,128)} %refs_4_.1), channel_id=1, source_target_pairs={{0,2},{1,3},{2,0},{3,1},{4,6},{5,7},{6,4},{7,5},{8,10},{9,11},{10,... | collective-permute-start | bytes 9224 | tf_op jit(solution)/shard_map/ppermute | solution.py:610
  5.6 5.7 %collective-permute-start.2 = (f32[4,8,24]{2,1,0:T(8,128)}, f32[4,8,24]{2,1,0:T(8,128)S(1)}, u32[]{:S(2)}, u32[]{:S(2)}) collective-permute-start(f32[4,8,24]{2,1,0:T(8,128)} %refs_4_.1), channel_id=1, source_target_pairs={{0,3},{1,2},{2,1},{3,0},{4,7},{5,6},{6,5},{7,4},{8,11},{9,10},{10,... | collective-permute-start | bytes 9224 | tf_op jit(solution)/shard_map/ppermute | solution.py:610
  9.2 6.7 %collective-permute-start.3 = (bf16[160,384]{1,0:T(8,128)(2,1)S(1)}, bf16[160,384]{1,0:T(8,128)(2,1)S(1)}, u32[]{:S(2)}, u32[]{:S(2)}) collective-permute-start(bf16[160,384]{1,0:T(8,128)(2,1)S(1)} %get-tuple-element.17.refs_1_), channel_id=1, source_target_pairs={{0,4},{4,0},{1,5},{5,1},{2,6},{6,2},{3,7},{7,3},{8,12},{12,8},{9,1... | collective-permute-start | bytes 368648 | tf_op jit(solution)/shard_map/ppermute | solution.py:600
  22.7 3.7 %collective-permute-start.4 = (f32[24,128]{1,0:T(8,128)S(1)}, f32[24,128]{1,0:T(8,128)S(1)}, u32[]{:S(2)}, u32[]{:S(2)}) collective-permute-start(f32[24,128]{1,0:T(8,128)S(1)} %shard_map.111), channel_id=1, source_target_pairs={{0,4},{4,0},{1,5},{5,1},{2,6},{6,2},{3,7},{7,3},{8,12},{12,8},{9,1... | collective-permute-start | bytes 36872 | tf_op jit(solution)/shard_map/ppermute | solution.py:655
  26.4 1.2 %collective-permute-start.5 = (f32[24,128]{1,0:T(8,128)S(1)}, f32[24,128]{1,0:T(8,128)S(1)}, u32[]{:S(2)}, u32[]{:S(2)}) collective-permute-start(f32[24,128]{1,0:T(8,128)S(1)} %add.12), channel_id=1, source_target_pairs={{0,8},{8,0},{16,24},{24,16},{1,9},{9,1},{17,25},{25,17},{2,10},{10... | collective-permute-start | bytes 36872 | tf_op jit(solution)/shard_map/ppermute | solution.py:655
  27.6 3.7 %collective-permute-start.6 = (f32[24,128]{1,0:T(8,128)S(1)}, f32[24,128]{1,0:T(8,128)S(1)}, u32[]{:S(2)}, u32[]{:S(2)}) collective-permute-start(f32[24,128]{1,0:T(8,128)S(1)} %add.13), channel_id=1, source_target_pairs={{0,16},{8,24},{16,0},{24,8},{1,17},{9,25},{17,1},{25,9},{2,18},{10... | collective-permute-start | bytes 36872 | tf_op jit(solution)/shard_map/ppermute | solution.py:655
  31.3 3.7 %collective-permute-start.7 = (f32[24,128]{1,0:T(8,128)S(1)}, f32[24,128]{1,0:T(8,128)S(1)}, u32[]{:S(2)}, u32[]{:S(2)}) collective-permute-start(f32[24,128]{1,0:T(8,128)S(1)} %add.14), channel_id=1, source_target_pairs={{0,1},{1,0},{2,3},{3,2},{4,5},{5,4},{6,7},{7,6},{8,9},{9,8},{10,11... | collective-permute-start | bytes 36872 | tf_op jit(solution)/shard_map/ppermute | solution.py:655
  35.0 4.6 %collective-permute-start.8 = (f32[24,128]{1,0:T(8,128)S(1)}, f32[24,128]{1,0:T(8,128)S(1)}, u32[]{:S(2)}, u32[]{:S(2)}) collective-permute-start(f32[24,128]{1,0:T(8,128)S(1)} %add.15.gram_a), channel_id=1, source_target_pairs={{0,2},{1,3},{2,0},{3,1},{4,6},{5,7},{6,4},{7,5},{8,10},{9,11},{10,... | collective-permute-start | bytes 36872 | tf_op jit(solution)/shard_map/ppermute | solution.py:655
